TPU v7x, 256 devices: a whole 4x4x8 slice. The times are simulated.
256 devices in a mesh: row: 16 (over y, x_lo, core), col: 16 (over x_hi, z).
Axes of the slice: x: 4 (x_hi: 2, x_lo: 2; x = x_hi * 2 + x_lo), y: 4, z: 8, core: 2. Of those that a mesh axis runs over, the one named last changes fastest.
Arguments:
- classes: int32 [256, 256], P('row', 'col'), may hold values from 0 to 15
- features: bfloat16 [256, 256, 128], P('row', 'col'), may hold values from -6 to 6
- cotangent: bfloat16 [256, 256, 128], P('row', 'col'), may hold values from -6 to 6
- table: float32 [16, 128], replicated, may hold values from -6 to 6
- norm_gain: float32 [128], replicated, may hold values from 0.5 to 1.5
- in_weight: bfloat16 [128, 512], replicated, may hold values from -0.5 to 0.5
- scan_weight: bfloat16 [256, 160], replicated, may hold values from -0.375 to 0.375
- step_weight: float32 [4, 8, 256], replicated, may hold values from -2 to 2
- step_bias: float32 [4, 256], replicated, may hold values from -6 to -2.5
- decay_log: float32 [4, 16, 256], replicated, may hold values from -4 to 2
- skip_gain: float32 [4, 256], replicated, may hold values from 0.5 to 1.5
- output_gain: float32 [256], replicated, may hold values from 0.5 to 1.5
- output_weight: bfloat16 [256, 128], replicated, may hold values from -0.375 to 0.375
Outputs:
- feature_grad: bfloat16 [256, 256, 128], P('row', 'col')
- in_weight_grad: float32 [128, 512], replicated
- scan_weight_grad: float32 [256, 160], replicated
- step_weight_grad: float32 [4, 8, 256], replicated
- step_bias_grad: float32 [4, 256], replicated
- decay_log_grad: float32 [4, 16, 256], replicated
- skip_gain_grad: float32 [4, 256], replicated
- norm_gain_grad: float32 [128], replicated
- output_gain_grad: float32 [256], replicated
- output_weight_grad: float32 [256, 128], replicated
All inputs are finite; a program needn't handle non-finite values.
Results may differ from a plain program's by a relative error of at most 0.0076.
Values sent between devices are 32-bit elements; how exact they have to be, the bound alone decides.
No kernel may reach another device: no remote copies, remote signals or barrier semaphores. Data moves between devices by JAX's collectives and lax.ppermute only.
A program may use at most 320 MiB of HBM per device.

v0:
```python
import functools

import jax
import jax.numpy as jnp
from jax import lax
from jax.experimental import pallas as pl
from jax.experimental.pallas import tpu as pltpu
from jax.sharding import PartitionSpec as P

EPS = 1e-05
HIGHEST = lax.Precision.HIGHEST
LOG2E = 1.4426950408889634
LN2 = 0.6931471805599453
CHUNKS = 8
LANES = 128
F32 = jnp.float32
BF16 = jnp.bfloat16
PARAMS = pltpu.CompilerParams(vmem_limit_bytes=48 * 1024 * 1024)


def normalise(rows):
    average = jnp.mean(rows, axis=-1, keepdims=True)
    centred = rows - average
    spread = jnp.mean(centred * centred, axis=-1, keepdims=True)
    inverse = lax.rsqrt(spread + EPS)
    return centred * inverse, inverse


def normalise_pull(upstream, unit, inverse):
    first = jnp.mean(upstream, axis=-1, keepdims=True)
    second = jnp.mean(upstream * unit, axis=-1, keepdims=True)
    return inverse * (upstream - first - unit * second)


def sigmoid(before):
    return 1.0 / (1.0 + jnp.exp(-before))


def softplus(before):
    return jnp.maximum(before, 0.0) + jnp.log1p(jnp.exp(-jnp.abs(before)))


def product(left, right, over=((1,), (0,)), precision=None):
    return lax.dot_general(left, right, (over, ((), ())), precision=precision, preferred_element_type=F32)


def embed_kernel(classes, features, table, embedded, turned, *, edge):
    labels = lax.broadcasted_iota(jnp.int32, (classes.shape[0], table.shape[0]), 1)
    onehot = (classes[...] == labels).astype(F32)
    cells = features[...].astype(F32) + product(onehot, table[...], precision=HIGHEST)
    embedded[...] = cells
    for row in range(edge):
        turned[pl.ds(row, edge, stride=edge), :] = cells[row * edge : (row + 1) * edge]


def chain_chunks(total, state, upward):
    place = lax.broadcasted_iota(jnp.int32, state.shape, 0)
    reach = 1
    while reach < CHUNKS:
        shift = reach if upward else CHUNKS - reach
        inside = place >= reach if upward else place < CHUNKS - reach
        state = state + total * jnp.where(inside, pltpu.roll(state, shift, 0), 0.0)
        total = total * jnp.where(inside, pltpu.roll(total, shift, 0), 1.0)
        reach *= 2
    shift = 1 if upward else CHUNKS - 1
    inside = place >= 1 if upward else place < CHUNKS - 1
    return jnp.where(inside, pltpu.roll(state, shift, 0), 0.0)


def spread_rates(decay_log, rates):
    for direction in range(2):
        scaled = -jnp.exp(decay_log[direction]) * LOG2E
        for entry in range(scaled.shape[0]):
            rates[direction, entry] = jnp.broadcast_to(
                scaled[entry : entry + 1], (CHUNKS, scaled.shape[1])
            )


def put_halves(target, rows):
    for half in range(target.shape[0]):
        target[half] = rows[:, half * LANES : (half + 1) * LANES]


def take_halves(source):
    return jnp.concatenate([source[half] for half in range(source.shape[0])], axis=1)


def load_interleaved(source):
    span = source.shape[0] // CHUNKS
    return jnp.concatenate(
        [source[pl.ds(place, CHUNKS, stride=span), :] for place in range(span)], axis=0
    )


def store_natural(target, rows):
    span = rows.shape[0] // CHUNKS
    for place in range(span):
        target[pl.ds(place, CHUNKS, stride=span), :] = rows[place * CHUNKS : (place + 1) * CHUNKS]


def sweep(span, advance, carried, unroll):
    def several(turn, state):
        for part in range(unroll):
            state = advance(turn * unroll + part, state)
        return state

    return lax.fori_loop(0, span // unroll, several, carried)


def expand_columns(flat, columns, rank, group):
    length, width = flat.shape
    wanted = group - rank
    padded = jnp.concatenate([flat, jnp.zeros((length, LANES - width), F32)], axis=1)
    high = padded.astype(BF16)
    low = (padded - high.astype(F32)).astype(BF16)
    both = jnp.concatenate([high, low], axis=1)
    row = lax.broadcasted_iota(jnp.int32, (2 * LANES, 2 * LANES), 0)
    lane = lax.broadcasted_iota(jnp.int32, (2 * LANES, 2 * LANES), 1)
    row = jnp.where(row >= LANES, row - LANES, row)
    offset = row - jnp.where(lane >= LANES, 1, 0)
    for direction in range(2):

        def one(pair, unused, direction=direction):
            chosen = (offset == direction * group + rank + 2 * pair).astype(F32).astype(BF16)
            wide = product(both, chosen)
            columns[direction * wanted + 2 * pair] = wide[:, :LANES]
            columns[direction * wanted + 2 * pair + 1] = wide[:, LANES:]
            return unused

        lax.fori_loop(0, wanted // 2, one, 0)


def sum_columns(terms, target, first):
    row = lax.broadcasted_iota(jnp.int32, (2 * LANES, LANES), 0)
    lane = lax.broadcasted_iota(jnp.int32, (2 * LANES, LANES), 1)
    offset = lane - jnp.where(row >= LANES, 1, 0)

    def one(pair, unused):
        chosen = (offset == first + 2 * pair).astype(F32).astype(BF16)
        both = jnp.concatenate([terms[2 * pair], terms[2 * pair + 1]], axis=1).astype(BF16)
        target[...] = target[...] + product(both, chosen)
        return unused

    lax.fori_loop(0, terms.shape[0] // 2, one, 0)


def slot(place):
    return pl.ds(pl.multiple_of(place * CHUNKS, CHUNKS), CHUNKS)


def forward_kernel(
    embedded,
    norm_gain,
    in_weight,
    scan_weight,
    step_weight,
    step_bias,
    decay_log,
    skip_gain,
    result,
    mixed_out,
    steps,
    projected,
    starts,
    values,
    rates,
    totals,
    natural,
    columns,
    *,
    rank,
    states,
):
    length, inner = result.shape
    halves = inner // LANES
    span = length // CHUNKS
    group = rank + 2 * states
    unit, unused = normalise(load_interleaved(embedded))
    normed = (unit * norm_gain[...]).astype(BF16)
    mixed = product(normed, in_weight[...])
    mixed_out[...] = mixed
    rounded = (mixed * sigmoid(mixed)).astype(BF16)
    flat = product(rounded, scan_weight[...])
    projected[...] = flat
    expand_columns(flat, columns, rank, group)
    wide = rounded.astype(F32)
    values[...] = wide
    totals[...] = wide * (skip_gain[0:1] + skip_gain[1:2])
    for direction in range(2):
        lowrank = flat[:, direction * group : direction * group + rank]
        before = (
            product(lowrank, step_weight[direction], precision=HIGHEST)
            + step_bias[direction : direction + 1]
        )
        steps[direction] = softplus(before)
    spread_rates(decay_log, rates)
    zero = jnp.zeros((CHUNKS, LANES), F32)

    for direction in range(2):
        source = direction * 2 * states
        probe = source + states

        def rows(turn, direction=direction):
            return slot(turn if direction == 0 else span - 1 - turn)

        for half in range(halves):
            lanes = slice(half * LANES, (half + 1) * LANES)

            def ending(turn, carried, direction=direction, lanes=lanes, rows=rows, source=source):
                state, total = carried
                at = rows(turn)
                step = steps[direction, at, lanes]
                drive = step * values[at, lanes]
                state = tuple(
                    jnp.exp2(step * rates[direction, n, :, lanes]) * state[n]
                    + columns[source + n, at, :] * drive
                    for n in range(states)
                )
                return (state, total + step)

            state, total = sweep(span, ending, ((zero,) * states, zero), 4)
            begin = []
            for n in range(states):
                factor = jnp.exp2(total * rates[direction, n, :, lanes])
                start = chain_chunks(factor, state[n], direction == 0)
                starts[direction, n, :, lanes] = start
                begin.append(start)

            def advance(
                turn, state, direction=direction, lanes=lanes, rows=rows, source=source, probe=probe
            ):
                at = rows(turn)
                step = steps[direction, at, lanes]
                drive = step * values[at, lanes]
                output = totals[at, lanes]
                after = []
                for n in range(states):
                    here = (
                        jnp.exp2(step * rates[direction, n, :, lanes]) * state[n]
                        + columns[source + n, at, :] * drive
                    )
                    output = output + columns[probe + n, at, :] * here
                    after.append(here)
                totals[at, lanes] = output
                return tuple(after)

            sweep(span, advance, tuple(begin), 4)
    for half in range(halves):
        store_natural(natural.at[half], totals[:, half * LANES : (half + 1) * LANES])
    result[...] = take_halves(natural)


def pack_sizes(inner, width, rank, states):
    halves = inner // LANES
    group = rank + 2 * states
    sizes = (halves * width, halves * 2 * group, halves * 2 * rank, halves * 2 * states, 8)
    firsts = [sum(sizes[:index]) for index in range(len(sizes) + 1)]
    return firsts


def pack_halves(target, first, rows):
    height, width = rows.shape
    for half in range(width // LANES):
        target[first + half * height : first + (half + 1) * height] = rows[
            :, half * LANES : (half + 1) * LANES
        ]


def gate_kernel(
    embedded,
    norm_gain,
    in_weight,
    output_gain,
    output_weight,
    cotangent,
    along_rows,
    along_cols,
    d_rows,
    d_cols,
    d_embedded,
    packed,
    turned,
    *,
    edge,
):
    inner, width = output_weight.shape
    halves = inner // LANES
    put_halves(turned, along_cols[...])
    total = along_rows[...] + jnp.concatenate(
        [
            jnp.concatenate(
                [turned[half, pl.ds(row, edge, stride=edge), :] for row in range(edge)], axis=0
            )
            for half in range(halves)
        ],
        axis=1,
    )
    base, inverse = normalise(embedded[...])
    gain = norm_gain[...]
    normed = (base * gain).astype(BF16)
    gate_in = product(normed, in_weight[...])
    sigma = sigmoid(gate_in)
    gate = gate_in * sigma
    slope = sigma * (1.0 + gate_in * (1.0 - sigma))
    unit, spread = normalise(total)
    strength = output_gain[...]
    gated = (unit * strength * gate).astype(BF16)
    upstream = cotangent[...]
    d_gated = product(upstream, output_weight[...], ((1,), (1,)))
    d_scaled = d_gated * gate
    d_total = normalise_pull(d_scaled * strength, unit, spread)
    d_rows[...] = d_total
    for half in range(halves):
        lanes = slice(half * LANES, (half + 1) * LANES)
        for row in range(edge):
            turned[half, pl.ds(row, edge, stride=edge), :] = d_total[
                row * edge : (row + 1) * edge, lanes
            ]
    d_cols[...] = take_halves(turned)
    d_gate = (d_gated * unit * strength * slope).astype(BF16)
    d_normed = product(d_gate, in_weight[...], ((1,), (1,)))
    d_embedded[...] = normalise_pull(d_normed * gain, base, inverse) + upstream.astype(F32)
    first = halves * width
    pack_halves(packed, 0, product(normed, d_gate, ((0,), (0,))))
    packed[first : first + inner] = product(gated, upstream, ((0,), (0,)))
    last = first + inner
    packed[last : last + 8] = jnp.zeros((8, LANES), F32)
    packed[last : last + 1] = jnp.sum(d_normed * base, axis=0, keepdims=True)
    pack_halves(packed, last + 1, jnp.sum(d_scaled * unit, axis=0, keepdims=True))


def backward_kernel(
    embedded,
    norm_gain,
    in_weight,
    scan_weight,
    step_weight,
    step_bias,
    decay_log,
    mixed_in,
    steps,
    projected,
    starts,
    upstream,
    skip_gain,
    d_embedded,
    packed,
    values,
    rates,
    history,
    decays,
    d_projected,
    d_values,
    d_steps,
    d_rates,
    enter,
    natural,
    arriving_lines,
    columns,
    terms,
    *,
    rank,
    states,
):
    length, inner = upstream.shape
    width = embedded.shape[1]
    halves = inner // LANES
    span = length // CHUNKS
    group = rank + 2 * states
    firsts = pack_sizes(inner, width, rank, states)
    mixed = mixed_in[...]
    sigma = sigmoid(mixed)
    rounded = (mixed * sigma).astype(BF16)
    wide = rounded.astype(F32)
    values[...] = wide
    put_halves(natural, upstream[...])
    incoming = jnp.concatenate(
        [load_interleaved(natural.at[half]) for half in range(halves)], axis=1
    )
    arriving_lines[...] = incoming
    d_values[...] = incoming * (skip_gain[0:1] + skip_gain[1:2])
    flat = projected[...]
    expand_columns(flat, columns, rank, group)
    d_projected[...] = jnp.zeros(d_projected.shape, F32)
    spread_rates(decay_log, rates)
    zero = jnp.zeros((CHUNKS, LANES), F32)
    packed[firsts[4] : firsts[5]] = jnp.zeros((8, LANES), F32)
    pack_halves(packed, firsts[4] + 1, jnp.sum(incoming * wide, axis=0, keepdims=True))

    for direction in range(2):
        source = direction * 2 * states
        probe = source + states
        d_rates[...] = jnp.zeros(d_rates.shape, F32)

        def rows(turn, direction=direction):
            return slot(turn if direction == 0 else span - 1 - turn)

        for half in range(halves):
            lanes = slice(half * LANES, (half + 1) * LANES)

            def advance(turn, carried, direction=direction, lanes=lanes, rows=rows, source=source):
                state, total = carried
                at = rows(turn)
                step = steps[direction, at, lanes]
                drive = step * values[at, lanes]
                after = []
                for n in range(states):
                    decay = jnp.exp2(step * rates[direction, n, :, lanes])
                    decays[turn, n, :, lanes] = decay
                    here = decay * state[n] + columns[source + n, at, :] * drive
                    history[turn + 1, n, :, lanes] = here
                    after.append(here)
                return (tuple(after), total + step)

            begin = tuple(starts[direction, n, :, lanes] for n in range(states))
            for n in range(states):
                history[0, n, :, lanes] = begin[n]
            unused, total = sweep(span, advance, (begin, zero), 4)

            def retreat(turn, carried, lanes=lanes, rows=rows, probe=probe):
                back = span - 1 - turn
                at = rows(back)
                arriving = arriving_lines[at, lanes]
                return tuple(
                    decays[back, n, :, lanes]
                    * (columns[probe + n, at, :] * arriving + carried[n])
                    for n in range(states)
                )

            carried = sweep(span, retreat, (zero,) * states, 4)
            for n in range(states):
                factor = jnp.exp2(total * rates[direction, n, :, lanes])
                enter[n, :, lanes] = chain_chunks(factor, carried[n], direction == 1)

        def pull(turn, carried, direction=direction, rows=rows, source=source, probe=probe):
            back = span - 1 - turn
            at = rows(back)
            step = steps[direction, at, :]
            value = values[at, :]
            drive = step * value
            arriving = arriving_lines[at, :]
            d_drive = jnp.zeros((CHUNKS, inner), F32)
            d_step = jnp.zeros((CHUNKS, inner), F32)
            after = []
            for n in range(states):
                reader = jnp.concatenate([columns[probe + n, at, :]] * halves, axis=1)
                writer = jnp.concatenate([columns[source + n, at, :]] * halves, axis=1)
                adjoint = reader * arriving + carried[n]
                leaving = decays[back, n] * adjoint
                after.append(leaving)
                d_probe = arriving * history[back + 1, n]
                d_source = adjoint * drive
                terms[n, at, :] = sum(
                    d_source[:, half * LANES : (half + 1) * LANES] for half in range(halves)
                )
                terms[states + n, at, :] = sum(
                    d_probe[:, half * LANES : (half + 1) * LANES] for half in range(halves)
                )
                d_drive = d_drive + adjoint * writer
                weight = leaving * history[back, n]
                d_step = d_step + weight * rates[direction, n]
                d_rates[n] = d_rates[n] + weight * step
            d_values[at, :] = d_values[at, :] + step * d_drive
            d_steps[at, :] = value * d_drive + LN2 * d_step
            return tuple(after)

        sweep(span, pull, tuple(enter[n] for n in range(states)), 1)
        first = direction * group
        sum_columns(terms, d_projected, first + rank)
        pack_halves(
            packed,
            firsts[3] + direction * halves * states,
            jnp.sum(d_rates[...], axis=1) * -jnp.exp(decay_log[direction]),
        )
        lowrank = flat[:, first : first + rank]
        before = (
            product(lowrank, step_weight[direction], precision=HIGHEST)
            + step_bias[direction : direction + 1]
        )
        d_before = d_steps[...] * sigmoid(before)
        pack_halves(
            packed,
            firsts[4] + 1 + halves * (1 + direction),
            jnp.sum(d_before, axis=0, keepdims=True),
        )
        pack_halves(
            packed,
            firsts[2] + direction * halves * rank,
            product(lowrank, d_before, ((0,), (0,)), HIGHEST),
        )
        d_projected[:, first : first + rank] = product(
            d_before, step_weight[direction], ((1,), (1,)), HIGHEST
        )

    unit, inverse = normalise(load_interleaved(embedded))
    gain = norm_gain[...]
    normed = (unit * gain).astype(BF16)
    d_flat = d_projected[:, : 2 * group].astype(BF16)
    pack_halves(packed, firsts[1], product(d_flat, rounded, ((0,), (0,))))
    d_all = product(d_flat, scan_weight[...], ((1,), (1,))) + d_values[...]
    d_mixed = (d_all * sigma * (1.0 + mixed * (1.0 - sigma))).astype(BF16)
    pack_halves(packed, 0, product(normed, d_mixed, ((0,), (0,))))
    d_normed = product(d_mixed, in_weight[...], ((1,), (1,)))
    packed[firsts[4] : firsts[4] + 1] = jnp.sum(d_normed * unit, axis=0, keepdims=True)
    store_natural(d_embedded, normalise_pull(d_normed * gain, unit, inverse))


def finish_kernel(own, along_rows, along_cols, gradient, turned, *, edge):
    turned[...] = along_cols[...].reshape(turned.shape)
    natural = jnp.concatenate(
        [turned[pl.ds(row, edge, stride=edge), :] for row in range(edge)], axis=0
    )
    gradient[...] = (own[...] + along_rows[...] + natural).astype(BF16)


def pack_kernel(gate, first, second, lines, blocks, stacked, *, shared):
    count, height, unused = blocks.shape
    edge = lines.shape[0] // count
    gate_rows, scan_rows = (gate.shape[0], first.shape[0])
    rest = scan_rows - shared
    stacked[:gate_rows] = gate[...]
    stacked[gate_rows : gate_rows + shared] = first[:shared] + second[:shared]
    start = gate_rows + shared
    stacked[start : start + rest] = first[shared:]
    stacked[start + rest : start + 2 * rest] = second[shared:]
    start = start + 2 * rest
    stacked[start:] = jnp.zeros((stacked.shape[0] - start, LANES), F32)
    for block in range(count):
        blocks[block, :edge] = lines[block * edge : (block + 1) * edge]
        blocks[block, edge:] = stacked[block * (height - edge) : (block + 1) * (height - edge)]


def unpack_kernel(
    whole,
    in_weight,
    scan_weight,
    step_weight,
    step_bias,
    decay,
    skip,
    norm_gain,
    output_gain,
    output_weight,
    *,
    scale,
    rank,
    states,
):
    width, double = in_weight.shape
    inner = double // 2
    halves = inner // LANES
    group = rank + 2 * states
    firsts = pack_sizes(inner, width, rank, states)
    shared = firsts[1]

    def joined(start, height):
        return scale * jnp.concatenate(
            [whole[start + half * height : start + (half + 1) * height] for half in range(halves)],
            axis=1,
        )

    gate = halves * width + inner + 8
    in_weight[:, inner:] = joined(0, width)
    in_weight[:, :inner] = joined(gate, width)
    output_weight[...] = scale * whole[halves * width : halves * width + inner]
    small = halves * width + inner
    output_gain[...] = joined(small + 1, 1)
    gains = whole[small : small + 1]
    projected = []
    for pair in range(2):
        start = gate + shared + pair * (firsts[5] - shared) - shared
        projected.append(joined(start + firsts[1], 2 * group))
        for direction in range(2):
            index = 2 * pair + direction
            step_weight[index] = joined(start + firsts[2] + direction * halves * rank, rank)
            decay[index] = joined(start + firsts[3] + direction * halves * states, states)
            base = start + firsts[4] + 1
            skip[index : index + 1] = joined(base, 1)
            step_bias[index : index + 1] = joined(base + halves * (1 + direction), 1)
        gains = gains + whole[start + firsts[4] : start + firsts[4] + 1]
    norm_gain[...] = scale * gains
    scan_weight[...] = jnp.concatenate(projected, axis=0).T


def shape_of(*sizes, dtype=F32):
    return jax.ShapeDtypeStruct(sizes, dtype)


def exchange(rows, axis):
    count = lax.axis_size(axis)
    length, width = rows.shape
    blocks = rows.reshape(count, length // count, width)
    return lax.all_to_all(blocks, axis, 0, 0).reshape(length, width)


def share(block, axis):
    count = lax.axis_size(axis)
    copies = jnp.broadcast_to(block[None], (count,) + block.shape)
    return lax.all_to_all(copies, axis, 0, 0)


def local(
    classes,
    features,
    cotangent,
    table,
    norm_gain,
    in_weight,
    scan_weight,
    step_weight,
    step_bias,
    decay_log,
    skip_gain,
    output_gain,
    output_weight,
):
    edge, across, width = features.shape
    inner = output_weight.shape[0]
    rank, states = (step_weight.shape[1], decay_log.shape[1])
    group = rank + 2 * states
    cells = edge * across
    span = cells // CHUNKS
    halves = inner // LANES
    scale = float(cells * lax.axis_size("row") * lax.axis_size("col")) ** (-0.5)
    gain = norm_gain.reshape(1, width)
    value_weight, gate_weight = (in_weight[:, :inner], in_weight[:, inner:])

    embedded, turned = pl.pallas_call(
        functools.partial(embed_kernel, edge=edge),
        out_shape=(shape_of(cells, width), shape_of(cells, width)),
        compiler_params=PARAMS,
        name="embed",
    )(classes.reshape(cells, 1), features.reshape(cells, width), table)

    forward = pl.pallas_call(
        functools.partial(forward_kernel, rank=rank, states=states),
        out_shape=(
            shape_of(cells, inner),
            shape_of(cells, inner),
            shape_of(2, cells, inner),
            shape_of(cells, 2 * group),
            shape_of(2, states, CHUNKS, inner),
        ),
        scratch_shapes=[
            pltpu.VMEM((cells, inner), F32),
            pltpu.VMEM((2, states, CHUNKS, inner), F32),
            pltpu.VMEM((cells, inner), F32),
            pltpu.VMEM((halves, cells, LANES), F32),
            pltpu.VMEM((4 * states, cells, LANES), F32),
        ],
        compiler_params=PARAMS,
        name="forward_scans",
    )
    axes = ("col", "row")
    lines = [exchange(embedded, "col"), exchange(turned, "row")]
    pairs = []
    for pair in range(2):
        two = slice(2 * pair, 2 * pair + 2)
        weights = (
            gain,
            value_weight,
            scan_weight[:, 2 * pair * group : 2 * (pair + 1) * group],
            step_weight[two],
            step_bias[two],
            decay_log[two],
        )
        pairs.append((weights, skip_gain[two]))
    kept, sums = ([], [])
    for pair in range(2):
        weights, skips = pairs[pair]
        outputs = forward(lines[pair], *weights, skips)
        kept.append(outputs[1:])
        sums.append(exchange(outputs[0], axes[pair]))

    firsts = pack_sizes(inner, width, rank, states)
    gate_rows = halves * width + inner + 8
    d_rows, d_cols, d_own, gate_packed = pl.pallas_call(
        functools.partial(gate_kernel, edge=edge),
        out_shape=(
            shape_of(cells, inner),
            shape_of(cells, inner),
            shape_of(cells, width),
            shape_of(gate_rows, LANES),
        ),
        scratch_shapes=[pltpu.VMEM((halves, cells, LANES), F32)],
        compiler_params=PARAMS,
        name="gate",
    )(
        embedded,
        gain,
        gate_weight,
        output_gain.reshape(1, inner),
        output_weight,
        cotangent.reshape(cells, width),
        sums[0],
        sums[1],
    )

    backward = pl.pallas_call(
        functools.partial(backward_kernel, rank=rank, states=states),
        out_shape=(shape_of(cells, width), shape_of(firsts[5], LANES)),
        scratch_shapes=[
            pltpu.VMEM((cells, inner), F32),
            pltpu.VMEM((2, states, CHUNKS, inner), F32),
            pltpu.VMEM((span + 1, states, CHUNKS, inner), F32),
            pltpu.VMEM((span, states, CHUNKS, inner), F32),
            pltpu.VMEM((cells, LANES), F32),
            pltpu.VMEM((cells, inner), F32),
            pltpu.VMEM((cells, inner), F32),
            pltpu.VMEM((states, CHUNKS, inner), F32),
            pltpu.VMEM((states, CHUNKS, inner), F32),
            pltpu.VMEM((halves, cells, LANES), F32),
            pltpu.VMEM((cells, inner), F32),
            pltpu.VMEM((4 * states, cells, LANES), F32),
            pltpu.VMEM((2 * states, cells, LANES), F32),
        ],
        compiler_params=PARAMS,
        name="backward_scans",
    )
    arriving = [exchange(d_rows, "col"), exchange(d_cols, "row")]
    outputs = []
    for pair in range(2):
        weights, skips = pairs[pair]
        outputs.append(backward(lines[pair], *weights, *kept[pair], arriving[pair], skips))
    returned = exchange(outputs[0][0], "col")

    row_count, col_count = (lax.axis_size("row"), lax.axis_size("col"))
    shared = firsts[1]
    stacked_rows = gate_rows + 2 * firsts[5] - shared
    stacked_rows += -stacked_rows % (row_count * 8)
    share_rows = stacked_rows // row_count
    blocks = pl.pallas_call(
        functools.partial(pack_kernel, shared=shared),
        out_shape=shape_of(row_count, edge + share_rows, LANES),
        scratch_shapes=[pltpu.VMEM((stacked_rows, LANES), F32)],
        compiler_params=PARAMS,
        name="pack",
    )(gate_packed, outputs[0][1], outputs[1][1], outputs[1][0])
    received = lax.all_to_all(blocks, "row", 0, 0)
    partial = jnp.sum(received[:, edge:], axis=0)
    partial = jnp.pad(partial, ((0, -share_rows % (col_count * 8)), (0, 0)))
    partial = partial.reshape(col_count, -1, LANES)
    owned = jnp.sum(lax.all_to_all(partial, "col", 0, 0), axis=0)
    column_sums = share(owned, "col").reshape(-1, LANES)[:share_rows]
    whole = share(column_sums, "row").reshape(stacked_rows, LANES)

    feature_grad = pl.pallas_call(
        functools.partial(finish_kernel, edge=edge),
        out_shape=shape_of(cells, width, dtype=BF16),
        scratch_shapes=[pltpu.VMEM((cells, width), F32)],
        compiler_params=PARAMS,
        name="finish",
    )(d_own, returned, received[:, :edge])
    grads = pl.pallas_call(
        functools.partial(unpack_kernel, scale=scale, rank=rank, states=states),
        out_shape=(
            shape_of(width, 2 * inner),
            shape_of(inner, 4 * group),
            shape_of(4, rank, inner),
            shape_of(4, inner),
            shape_of(4, states, inner),
            shape_of(4, inner),
            shape_of(1, width),
            shape_of(1, inner),
            shape_of(inner, width),
        ),
        compiler_params=PARAMS,
        name="unpack",
    )(whole)
    return (
        feature_grad.reshape(edge, across, width),
        *grads[:6],
        grads[6].reshape(width),
        grads[7].reshape(inner),
        grads[8],
    )


def solution(mesh):
    tiled = P("row", "col", None)
    in_specs = (P("row", "col"), tiled, tiled) + (P(),) * 10
    out_specs = (tiled,) + (P(),) * 9
    return jax.shard_map(local, mesh=mesh, in_specs=in_specs, out_specs=out_specs, check_vma=False)
```

profile of v0, /device:TPU:1, one launch (start us, length us, event | category | flops | bytes accessed | tf_op | source)
XLA Modules:
  0.0 234.3 jit_solution(13209238234534768721)
XLA Ops:
  1.5 1.0 embed.1
  2.6 7.0 %all-to-all-start.2 = ((f32[16,16,128]{2,1,0:T(8,128)}), f32[16,16,128]{2,1,0:T(8,128)S(1)}, u32[]{:S(2)}, u32[]{:S(2)}) async-start(f32[16,16,128]{2,1,0:T(8,128)} %bitcast.8), calls=%async_computation.2 | async-start | bytes 262144 | tf_op jit(solution)/shard_map/all_to_all | solution.py:593
  11.3 4.5 %all-to-all-done.2 = f32[16,16,128]{2,1,0:T(8,128)S(1)} async-done(((f32[16,16,128]{2,1,0:T(8,128)}), f32[16,16,128]{2,1,0:T(8,128)S(1)}, u32[]{:S(2)}, u32[]{:S(2)}) %all-to-all-start.2) | async-done | bytes 131104 | tf_op jit(solution)/shard_map/all_to_all | solution.py:593
  15.8 10.6 %all-to-all-start = ((f32[16,16,128]{2,1,0:T(8,128)}), f32[16,16,128]{2,1,0:T(8,128)S(1)}, u32[]{:S(2)}, u32[]{:S(2)}) async-start(f32[16,16,128]{2,1,0:T(8,128)} %bitcast.4), calls=%async_computation | async-start | bytes 262144 | tf_op jit(solution)/shard_map/all_to_all | solution.py:593
  27.2 13.7 %forward_scans.3 = (f32[256,256]{1,0:T(8,128)}, f32[256,256]{1,0:T(8,128)S(1)}, f32[2,256,256]{2,1,0:T(8,128)S(1)}, f32[256,80]{1,0:T(8,128)S(1)}, f32[2,16,8,256]{3,2,1,0:T(8,128)S(1)}) custom-call(f32[256,128]{1,0:T(8,128)S(1)} %bitcast.29, f32[1,128]{1,0:T(1,128)S(1)} %bitcast.40, bf16[128,256]{1,0:T(8,128)(2,1)S(1)} %get-tuple-element.98.in_weight, ...), custom_call_target="tpu_custom_call" | custom-call | tf_op jit(solution)/shard_map/forward_scans/pallas_call | solution.py:671
  41.5 4.3 %all-to-all-start.3 = ((f32[16,16,256]{2,1,0:T(8,128)}), f32[16,16,256]{2,1,0:T(8,128)S(1)}, u32[]{:S(2)}, u32[]{:S(2)}) async-start(f32[16,16,256]{2,1,0:T(8,128)} %bitcast.10), calls=%async_computation.3 | async-start | bytes 524288 | tf_op jit(solution)/shard_map/all_to_all | solution.py:593
  45.9 13.0 %forward_scans.2 = (f32[256,256]{1,0:T(8,128)S(1)}, f32[256,256]{1,0:T(8,128)S(1)}, f32[2,256,256]{2,1,0:T(8,128)S(1)}, f32[256,80]{1,0:T(8,128)S(1)}, f32[2,16,8,256]{3,2,1,0:T(8,128)S(1)}) custom-call(f32[256,128]{1,0:T(8,128)S(1)} %bitcast.27, f32[1,128]{1,0:T(1,128)S(1)} %bitcast.41, bf16[128,256]{1,0:T(8,128)(2,1)S(1)} %get-tuple-element.98.in_weight, ...), custom_call_target="tpu_custom_call" | custom-call | tf_op jit(solution)/shard_map/forward_scans/pallas_call | solution.py:671
  59.5 19.9 %all_to_all.55 = f32[16,16,256]{2,1,0:T(8,128)S(1)} all-to-all(f32[16,16,256]{2,1,0:T(8,128)S(1)} %bitcast.36), channel_id=1, replica_groups=mesh['row'=16,'col'=16] {'col'}, dimensions={0} | all-to-all | bytes 524288 | tf_op jit(solution)/shard_map/all_to_all | solution.py:593
  80.1 2.4 %gate.1 = (f32[256,256]{1,0:T(8,128)}, f32[256,256]{1,0:T(8,128)S(1)}, f32[256,128]{1,0:T(8,128)S(1)}, f32[520,128]{1,0:T(8,128)S(1)}) custom-call(f32[256,128]{1,0:T(8,128)} %get-tuple-element.39.embedded, f32[1,128]{1,0:T(1,128)S(1)} %bitcast.42, bf16[128,256]{1,0:T(8,128)(2,1)S(1)} %get-tuple-element.99.in_weight, f32[1,256]{1,0:T(1,128)S(1)} %bitcast.45, ...), custom_call_target="tpu_custom_call" | custom-call | tf_op jit(solution)/shard_map/gate/pallas_call | solution.py:677
  82.5 13.8 %all_to_all.56 = f32[16,16,256]{2,1,0:T(8,128)S(1)} all-to-all(f32[16,16,256]{2,1,0:T(8,128)S(1)} %bitcast.37), channel_id=1, replica_groups=mesh['row'=16,'col'=16] {'row'}, dimensions={0} | all-to-all | bytes 524288 | tf_op jit(solution)/shard_map/all_to_all | solution.py:593
  96.2 4.8 %all-to-all-start.4 = ((f32[16,16,256]{2,1,0:T(8,128)}), f32[16,16,256]{2,1,0:T(8,128)S(1)}, u32[]{:S(2)}, u32[]{:S(2)}) async-start(f32[16,16,256]{2,1,0:T(8,128)} %bitcast.12), calls=%async_computation.4 | async-start | bytes 524288 | tf_op jit(solution)/shard_map/all_to_all | solution.py:593
  101.1 0.9 copy-done.7
  102.0 23.4 %backward_scans.3 = (f32[256,128]{1,0:T(8,128)S(1)}, f32[520,128]{1,0:T(8,128)S(1)}) custom-call(f32[256,128]{1,0:T(8,128)S(1)} %bitcast.30, f32[1,128]{1,0:T(1,128)S(1)} %bitcast.43, bf16[128,256]{1,0:T(8,128)(2,1)S(1)} %get-tuple-element.98.in_weight, bf16[256,80]{1,0:T(8,128)(2,1)S(1)} %copy.35.scan_weight, ...), custom_call_target="tpu_custom_call" | custom-call | tf_op jit(solution)/shard_map/backward_scans/pallas_call | solution.py:724
  126.1 0.9 copy-done.1
  127.0 0.9 copy-done.9
  127.9 24.1 %backward_scans.2 = (f32[256,128]{1,0:T(8,128)}, f32[520,128]{1,0:T(8,128)S(1)}) custom-call(f32[256,128]{1,0:T(8,128)S(1)} %bitcast.28, f32[1,128]{1,0:T(1,128)S(1)} %bitcast.44, bf16[128,256]{1,0:T(8,128)(2,1)S(1)} %get-tuple-element.98.in_weight, bf16[256,80]{1,0:T(8,128)(2,1)S(1)} %copy.34.scan_weight, f32[2,8,256]{2,1,0:T(8,128)S(1)} %get-tuple-element.105.step_weight, ...), custom_call_target="tpu_custom_call" | custom-call | tf_op jit(solution)/shard_map/backward_scans/pallas_call | solution.py:724
  152.1 17.1 %all_to_all.57 = f32[16,104,128]{2,1,0:T(8,128)S(1)} all-to-all(f32[16,104,128]{2,1,0:T(8,128)S(1)} %pack.1), channel_id=1, replica_groups=mesh['row'=16,'col'=16] {'row'}, dimensions={0} | all-to-all | bytes 1703936 | tf_op jit(solution)/shard_map/all_to_all | solution.py:739
  169.3 18.0 %all_to_all.58 = f32[16,8,128]{2,1,0:T(8,128)S(1)} all-to-all(f32[16,8,128]{2,1,0:T(8,128)S(1)} %pad_bitcast_fusion), channel_id=1, replica_groups=mesh['row'=16,'col'=16] {'col'}, dimensions={0} | all-to-all | bytes 131072 | tf_op jit(solution)/shard_map/all_to_all | solution.py:743
  187.3 11.5 %all_to_all.59 = f32[16,8,128]{2,1,0:T(8,128)S(1)} all-to-all(f32[16,8,128]{2,1,0:T(8,128)S(1)} %broadcast_in_dim.6), channel_id=1, replica_groups=mesh['row'=16,'col'=16] {'col'}, dimensions={0} | all-to-all | bytes 131072 | tf_op jit(solution)/shard_map/all_to_all | solution.py:599
  198.8 3.5 %all-to-all-start.5 = ((f32[16,16,128]{2,1,0:T(8,128)}), f32[16,16,128]{2,1,0:T(8,128)S(1)}, u32[]{:S(2)}, u32[]{:S(2)}) async-start(f32[16,16,128]{2,1,0:T(8,128)} %bitcast.14), calls=%async_computation.5 | async-start | bytes 262144 | tf_op jit(solution)/shard_map/all_to_all | solution.py:593
  202.3 8.9 %all-to-all-done.5 = f32[16,16,128]{2,1,0:T(8,128)S(1)} async-done(((f32[16,16,128]{2,1,0:T(8,128)}), f32[16,16,128]{2,1,0:T(8,128)S(1)}, u32[]{:S(2)}, u32[]{:S(2)}) %all-to-all-start.5) | async-done | bytes 131104 | tf_op jit(solution)/shard_map/all_to_all | solution.py:593
  211.2 0.9 broadcast_in_dim.16
  212.1 8.3 %all-to-all-start.10 = ((f32[16,88,128]{2,1,0:T(8,128)}), f32[16,88,128]{2,1,0:T(8,128)S(1)}, u32[]{:S(2)}, u32[]{:S(2)}) async-start(f32[16,88,128]{2,1,0:T(8,128)} %broadcast_in_dim.16), calls=%async_computation.10 | async-start | bytes 1441792 | tf_op jit(solution)/shard_map/all_to_all | solution.py:599
  222.0 10.8 %all-to-all-done.10 = f32[16,88,128]{2,1,0:T(8,128)S(1)} async-done(((f32[16,88,128]{2,1,0:T(8,128)}), f32[16,88,128]{2,1,0:T(8,128)S(1)}, u32[]{:S(2)}, u32[]{:S(2)}) %all-to-all-start.10) | async-done | bytes 720928 | tf_op jit(solution)/shard_map/all_to_all | solution.py:599
  (62 shorter events, 9.4 us)
Async XLA Ops:
  0.6 0.9 copy-start.14
  0.7 0.9 copy-start.10
  2.6 7.0 %copy-start.18 = (f32[4,16,256]{2,1,0:T(8,128)S(1)}, f32[4,16,256]{2,1,0:T(8,128)}, u32[]{:S(2)}) copy-start(f32[4,16,256]{2,1,0:T(8,128)} %param.22) | copy-start | bytes 196612
  2.6 13.2 %all-to-all-start.2 = ((f32[16,16,128]{2,1,0:T(8,128)}), f32[16,16,128]{2,1,0:T(8,128)S(1)}, u32[]{:S(2)}, u32[]{:S(2)}) async-start(f32[16,16,128]{2,1,0:T(8,128)} %bitcast.8), calls=%async_computation.2 | async-start | bytes 262144 | tf_op jit(solution)/shard_map/all_to_all | solution.py:593
  9.6 0.9 copy-start.17
  10.5 0.8 copy-start.19
  15.7 10.6 %copy-start.20 = (f32[4,256]{1,0:T(4,128)S(1)}, f32[4,256]{1,0:T(4,128)}, u32[]{:S(2)}) copy-start(f32[4,256]{1,0:T(4,128)} %param.23) | copy-start | bytes 12292
  15.7 10.6 %copy-start.21 = (f32[4,256]{1,0:T(4,128)S(1)}, f32[4,256]{1,0:T(4,128)}, u32[]{:S(2)}) copy-start(f32[4,256]{1,0:T(4,128)} %param.21) | copy-start | bytes 12292
  15.7 10.8 %copy-start.16 = (bf16[128,512]{1,0:T(8,128)(2,1)S(1)}, bf16[128,512]{1,0:T(8,128)(2,1)}, u32[]{:S(2)}) copy-start(bf16[128,512]{1,0:T(8,128)(2,1)} %param.18) | copy-start | bytes 393220
  15.8 25.1 %all-to-all-start = ((f32[16,16,128]{2,1,0:T(8,128)}), f32[16,16,128]{2,1,0:T(8,128)S(1)}, u32[]{:S(2)}, u32[]{:S(2)}) async-start(f32[16,16,128]{2,1,0:T(8,128)} %bitcast.4), calls=%async_computation | async-start | bytes 262144 | tf_op jit(solution)/shard_map/all_to_all | solution.py:593
  41.5 18.0 %all-to-all-start.3 = ((f32[16,16,256]{2,1,0:T(8,128)}), f32[16,16,256]{2,1,0:T(8,128)S(1)}, u32[]{:S(2)}, u32[]{:S(2)}) async-start(f32[16,16,256]{2,1,0:T(8,128)} %bitcast.10), calls=%async_computation.3 | async-start | bytes 524288 | tf_op jit(solution)/shard_map/all_to_all | solution.py:593
  59.5 19.9 %copy-start = (f32[2,16,8,256]{3,2,1,0:T(8,128)}, f32[2,16,8,256]{3,2,1,0:T(8,128)S(1)}, u32[]{:S(2)}) copy-start(f32[2,16,8,256]{3,2,1,0:T(8,128)S(1)} %get-tuple-element.47.starts) | copy-start | bytes 786436
  59.5 19.9 %copy-start.11 = (bf16[256,128]{1,0:T(8,128)(2,1)S(1)}, bf16[256,128]{1,0:T(8,128)(2,1)}, u32[]{:S(2)}) copy-start(bf16[256,128]{1,0:T(8,128)(2,1)} %output_weight.1) | copy-start | bytes 196612
  59.5 19.9 %copy-start.12 = (bf16[16,16,128]{2,1,0:T(8,128)(2,1)S(1)}, bf16[16,16,128]{2,1,0:T(8,128)(2,1)}, u32[]{:S(2)}) copy-start(bf16[16,16,128]{2,1,0:T(8,128)(2,1)} %param.15) | copy-start | bytes 196612
  79.4 0.7 copy-start.15
  82.5 13.8 %copy-start.2 = (f32[256,128]{1,0:T(8,128)}, f32[256,128]{1,0:T(8,128)S(1)}, u32[]{:S(2)}) copy-start(f32[256,128]{1,0:T(8,128)S(1)} %get-tuple-element.43.own) | copy-start | bytes 393220
  96.2 29.8 %all-to-all-start.4 = ((f32[16,16,256]{2,1,0:T(8,128)}), f32[16,16,256]{2,1,0:T(8,128)S(1)}, u32[]{:S(2)}, u32[]{:S(2)}) async-start(f32[16,16,256]{2,1,0:T(8,128)} %bitcast.12), calls=%async_computation.4 | async-start | bytes 524288 | tf_op jit(solution)/shard_map/all_to_all | solution.py:593
  101.1 0.9 copy-start.7
  126.1 1.0 copy-start.1
  127.0 0.9 copy-start.9
  127.9 24.1 %copy-start.5 = (f32[256,128]{1,0:T(8,128)S(1)}, f32[256,128]{1,0:T(8,128)}, u32[]{:S(2)}) copy-start(f32[256,128]{1,0:T(8,128)} %copy-done.4) | copy-start | bytes 393220
  198.8 12.4 %all-to-all-start.5 = ((f32[16,16,128]{2,1,0:T(8,128)}), f32[16,16,128]{2,1,0:T(8,128)S(1)}, u32[]{:S(2)}, u32[]{:S(2)}) async-start(f32[16,16,128]{2,1,0:T(8,128)} %bitcast.14), calls=%async_computation.5 | async-start | bytes 262144 | tf_op jit(solution)/shard_map/all_to_all | solution.py:593
  212.1 20.6 %all-to-all-start.10 = ((f32[16,88,128]{2,1,0:T(8,128)}), f32[16,88,128]{2,1,0:T(8,128)S(1)}, u32[]{:S(2)}, u32[]{:S(2)}) async-start(f32[16,88,128]{2,1,0:T(8,128)} %broadcast_in_dim.16), calls=%async_computation.10 | async-start | bytes 1441792 | tf_op jit(solution)/shard_map/all_to_all | solution.py:599
  220.4 0.9 copy-start.3
  (4 other events, 2.6 us)
where the time goes:
time: 235 us; the launch traced here: 234 us
  blocking collectives  80.2 us (34%)
  Pallas kernels  79.2 us (34%)
  starting transfers between devices  38.5 us (16%)
  waiting for transfers between devices  24.1 us (10%)
  local copies, waits for them, and re-layouts  11.4 us (5%)
    pallas_call x2, Pallas kernels, local(): backward(lines[pair], *weights, *kept[pair], arriving[pair], skips)  47.6 us
    all_to_all x2, blocking collectives, exchange(): return lax.all_to_all(blocks, axis, 0, 0).reshape(length, width)  33.6 us
    all_to_all x5, starting transfers between devices, exchange(): return lax.all_to_all(blocks, axis, 0, 0).reshape(length, width)  30.2 us
    pallas_call x2, Pallas kernels, local(): outputs = forward(lines[pair], *weights, skips)  26.6 us
    all_to_all x1, blocking collectives, local(): owned = jnp.sum(lax.all_to_all(partial, 'col', 0, 0), axis=0)  18 us
    all_to_all x1, blocking collectives, local(): received = lax.all_to_all(blocks, 'row', 0, 0)  17.1 us
    all_to_all x5, waiting for transfers between devices, exchange(): return lax.all_to_all(blocks, axis, 0, 0).reshape(length, width)  13.4 us
    all_to_all x1, blocking collectives, share(): return lax.all_to_all(copies, axis, 0, 0)  11.5 us
  transfers between devices with their start and end apart: 6, of which 3 were waited for; matrix products, arithmetic and copies ran while one was open for 0% of the time, Pallas kernels for 22%

commit v1 on v0

--- a/solution.py
+++ b/solution.py
@@ -15,7 +15,9 @@
 LANES = 128
 F32 = jnp.float32
 BF16 = jnp.bfloat16
-PARAMS = pltpu.CompilerParams(vmem_limit_bytes=48 * 1024 * 1024)
+SMALL = pltpu.CompilerParams(vmem_limit_bytes=12 * 1024 * 1024)
+MIDDLE = pltpu.CompilerParams(vmem_limit_bytes=20 * 1024 * 1024)
+LARGE = pltpu.CompilerParams(vmem_limit_bytes=36 * 1024 * 1024)
 
 
 def normalise(rows):
@@ -67,9 +69,9 @@
     return jnp.where(inside, pltpu.roll(state, shift, 0), 0.0)
 
 
-def spread_rates(decay_log, rates):
+def spread_rates(decay_log, rates, pair):
     for direction in range(2):
-        scaled = -jnp.exp(decay_log[direction]) * LOG2E
+        scaled = -jnp.exp(decay_log[2 * pair + direction]) * LOG2E
         for entry in range(scaled.shape[0]):
             rates[direction, entry] = jnp.broadcast_to(
                 scaled[entry : entry + 1], (CHUNKS, scaled.shape[1])
@@ -116,36 +118,79 @@
     both = jnp.concatenate([high, low], axis=1)
     row = lax.broadcasted_iota(jnp.int32, (2 * LANES, 2 * LANES), 0)
     lane = lax.broadcasted_iota(jnp.int32, (2 * LANES, 2 * LANES), 1)
-    row = jnp.where(row >= LANES, row - LANES, row)
-    offset = row - jnp.where(lane >= LANES, 1, 0)
+    odd_lane = (lane >= LANES).astype(jnp.int32)
+    copies = (row % 2 == odd_lane).astype(F32).astype(BF16)
+    place = lax.broadcasted_iota(jnp.int32, (1, 2 * LANES), 1) % LANES // 2
     for direction in range(2):
 
         def one(pair, unused, direction=direction):
-            chosen = (offset == direction * group + rank + 2 * pair).astype(F32).astype(BF16)
-            wide = product(both, chosen)
+            chosen = (place == (direction * group + rank) // 2 + pair).astype(F32).astype(BF16)
+            wide = product(both * chosen, copies)
             columns[direction * wanted + 2 * pair] = wide[:, :LANES]
             columns[direction * wanted + 2 * pair + 1] = wide[:, LANES:]
             return unused
 
-        lax.fori_loop(0, wanted // 2, one, 0)
+        sweep(wanted // 2, one, 0, 8)
 
 
 def sum_columns(terms, target, first):
     row = lax.broadcasted_iota(jnp.int32, (2 * LANES, LANES), 0)
     lane = lax.broadcasted_iota(jnp.int32, (2 * LANES, LANES), 1)
-    offset = lane - jnp.where(row >= LANES, 1, 0)
+    copies = (lane % 2 == (row >= LANES).astype(jnp.int32)).astype(F32).astype(BF16)
+    place = lax.broadcasted_iota(jnp.int32, target.shape, 1) // 2
 
     def one(pair, unused):
-        chosen = (offset == first + 2 * pair).astype(F32).astype(BF16)
         both = jnp.concatenate([terms[2 * pair], terms[2 * pair + 1]], axis=1).astype(BF16)
-        target[...] = target[...] + product(both, chosen)
+        target[...] = jnp.where(place == first // 2 + pair, product(both, copies), target[...])
         return unused
 
-    lax.fori_loop(0, terms.shape[0] // 2, one, 0)
+    sweep(terms.shape[0] // 2, one, 0, 4)
 
 
 def slot(place):
     return pl.ds(pl.multiple_of(place * CHUNKS, CHUNKS), CHUNKS)
+
+
+def pair_sum(gains, pair):
+    return gains[2 * pair : 2 * pair + 1] + gains[2 * pair + 1 : 2 * pair + 2]
+
+
+def line_inputs(
+    embedded,
+    norm_gain,
+    in_weight,
+    scan_weight,
+    step_weight,
+    step_bias,
+    targets,
+    pair,
+    rank,
+    group,
+):
+    steps, values, columns = targets
+    inner = values.shape[1]
+    unit, inverse = normalise(load_interleaved(embedded))
+    normed = (unit * norm_gain[...]).astype(BF16)
+    mixed = product(normed, in_weight[:, :inner])
+    sigma = sigmoid(mixed)
+    rounded = (mixed * sigma).astype(BF16)
+    flat = product(rounded, pair_rows(scan_weight, pair, group), ((1,), (1,)))
+    expand_columns(flat, columns, rank, group)
+    values[...] = rounded.astype(F32)
+    lowranks, before = ([], [])
+    for direction in range(2):
+        index = 2 * pair + direction
+        lowrank = flat[:, direction * group : direction * group + rank]
+        lowranks.append(lowrank)
+        before.append(
+            product(lowrank, step_weight[index], precision=HIGHEST) + step_bias[index : index + 1]
+        )
+        steps[direction] = softplus(before[direction])
+    return unit, inverse, normed, mixed, sigma, rounded, lowranks, before
+
+
+def pair_rows(scan_weight, pair, group):
+    return scan_weight[2 * pair * group : 2 * (pair + 1) * group]
 
 
 def forward_kernel(
@@ -158,16 +203,15 @@
     decay_log,
     skip_gain,
     result,
-    mixed_out,
+    starts,
     steps,
-    projected,
-    starts,
     values,
     rates,
     totals,
     natural,
     columns,
     *,
+    pair,
     rank,
     states,
 ):
@@ -175,25 +219,20 @@
     halves = inner // LANES
     span = length // CHUNKS
     group = rank + 2 * states
-    unit, unused = normalise(load_interleaved(embedded))
-    normed = (unit * norm_gain[...]).astype(BF16)
-    mixed = product(normed, in_weight[...])
-    mixed_out[...] = mixed
-    rounded = (mixed * sigmoid(mixed)).astype(BF16)
-    flat = product(rounded, scan_weight[...])
-    projected[...] = flat
-    expand_columns(flat, columns, rank, group)
-    wide = rounded.astype(F32)
-    values[...] = wide
-    totals[...] = wide * (skip_gain[0:1] + skip_gain[1:2])
-    for direction in range(2):
-        lowrank = flat[:, direction * group : direction * group + rank]
-        before = (
-            product(lowrank, step_weight[direction], precision=HIGHEST)
-            + step_bias[direction : direction + 1]
-        )
-        steps[direction] = softplus(before)
-    spread_rates(decay_log, rates)
+    unused = line_inputs(
+        embedded,
+        norm_gain,
+        in_weight,
+        scan_weight,
+        step_weight,
+        step_bias,
+        (steps, values, columns),
+        pair,
+        rank,
+        group,
+    )
+    totals[...] = values[...] * pair_sum(skip_gain, pair)
+    spread_rates(decay_log, rates, pair)
     zero = jnp.zeros((CHUNKS, LANES), F32)
 
     for direction in range(2):
@@ -218,7 +257,7 @@
                 )
                 return (state, total + step)
 
-            state, total = sweep(span, ending, ((zero,) * states, zero), 4)
+            state, total = sweep(span, ending, ((zero,) * states, zero), 8)
             begin = []
             for n in range(states):
                 factor = jnp.exp2(total * rates[direction, n, :, lanes])
@@ -244,7 +283,7 @@
                 totals[at, lanes] = output
                 return tuple(after)
 
-            sweep(span, advance, tuple(begin), 4)
+            sweep(span, advance, tuple(begin), 8)
     for half in range(halves):
         store_natural(natural.at[half], totals[:, half * LANES : (half + 1) * LANES])
     result[...] = take_halves(natural)
@@ -298,7 +337,8 @@
     base, inverse = normalise(embedded[...])
     gain = norm_gain[...]
     normed = (base * gain).astype(BF16)
-    gate_in = product(normed, in_weight[...])
+    gate_weight = in_weight[:, inner:]
+    gate_in = product(normed, gate_weight)
     sigma = sigmoid(gate_in)
     gate = gate_in * sigma
     slope = sigma * (1.0 + gate_in * (1.0 - sigma))
@@ -318,7 +358,7 @@
             ]
     d_cols[...] = take_halves(turned)
     d_gate = (d_gated * unit * strength * slope).astype(BF16)
-    d_normed = product(d_gate, in_weight[...], ((1,), (1,)))
+    d_normed = product(d_gate, gate_weight, ((1,), (1,)))
     d_embedded[...] = normalise_pull(d_normed * gain, base, inverse) + upstream.astype(F32)
     first = halves * width
     pack_halves(packed, 0, product(normed, d_gate, ((0,), (0,))))
@@ -337,14 +377,12 @@
     step_weight,
     step_bias,
     decay_log,
-    mixed_in,
-    steps,
-    projected,
+    skip_gain,
     starts,
     upstream,
-    skip_gain,
     d_embedded,
     packed,
+    steps,
     values,
     rates,
     history,
@@ -358,7 +396,9 @@
     arriving_lines,
     columns,
     terms,
+    slopes,
     *,
+    pair,
     rank,
     states,
 ):
@@ -368,24 +408,32 @@
     span = length // CHUNKS
     group = rank + 2 * states
     firsts = pack_sizes(inner, width, rank, states)
-    mixed = mixed_in[...]
-    sigma = sigmoid(mixed)
-    rounded = (mixed * sigma).astype(BF16)
-    wide = rounded.astype(F32)
-    values[...] = wide
+    gain = norm_gain[...]
+    unit, inverse, normed, mixed, sigma, rounded, lowranks, before = line_inputs(
+        embedded,
+        norm_gain,
+        in_weight,
+        scan_weight,
+        step_weight,
+        step_bias,
+        (steps, values, columns),
+        pair,
+        rank,
+        group,
+    )
+    for direction in range(2):
+        slopes[direction] = sigmoid(before[direction])
     put_halves(natural, upstream[...])
     incoming = jnp.concatenate(
         [load_interleaved(natural.at[half]) for half in range(halves)], axis=1
     )
     arriving_lines[...] = incoming
-    d_values[...] = incoming * (skip_gain[0:1] + skip_gain[1:2])
-    flat = projected[...]
-    expand_columns(flat, columns, rank, group)
+    d_values[...] = incoming * pair_sum(skip_gain, pair)
     d_projected[...] = jnp.zeros(d_projected.shape, F32)
-    spread_rates(decay_log, rates)
+    spread_rates(decay_log, rates, pair)
     zero = jnp.zeros((CHUNKS, LANES), F32)
     packed[firsts[4] : firsts[5]] = jnp.zeros((8, LANES), F32)
-    pack_halves(packed, firsts[4] + 1, jnp.sum(incoming * wide, axis=0, keepdims=True))
+    pack_halves(packed, firsts[4] + 1, jnp.sum(incoming * values[...], axis=0, keepdims=True))
 
     for direction in range(2):
         source = direction * 2 * states
@@ -427,7 +475,7 @@
                     for n in range(states)
                 )
 
-            carried = sweep(span, retreat, (zero,) * states, 4)
+            carried = sweep(span, retreat, (zero,) * states, 8)
             for n in range(states):
                 factor = jnp.exp2(total * rates[direction, n, :, lanes])
                 enter[n, :, lanes] = chain_chunks(factor, carried[n], direction == 1)
@@ -464,20 +512,15 @@
             d_steps[at, :] = value * d_drive + LN2 * d_step
             return tuple(after)
 
-        sweep(span, pull, tuple(enter[n] for n in range(states)), 1)
+        sweep(span, pull, tuple(enter[n] for n in range(states)), 2)
         first = direction * group
         sum_columns(terms, d_projected, first + rank)
         pack_halves(
             packed,
             firsts[3] + direction * halves * states,
-            jnp.sum(d_rates[...], axis=1) * -jnp.exp(decay_log[direction]),
+            jnp.sum(d_rates[...], axis=1) * -jnp.exp(decay_log[2 * pair + direction]),
         )
-        lowrank = flat[:, first : first + rank]
-        before = (
-            product(lowrank, step_weight[direction], precision=HIGHEST)
-            + step_bias[direction : direction + 1]
-        )
-        d_before = d_steps[...] * sigmoid(before)
+        d_before = d_steps[...] * slopes[direction]
         pack_halves(
             packed,
             firsts[4] + 1 + halves * (1 + direction),
@@ -486,21 +529,18 @@
         pack_halves(
             packed,
             firsts[2] + direction * halves * rank,
-            product(lowrank, d_before, ((0,), (0,)), HIGHEST),
+            product(lowranks[direction], d_before, ((0,), (0,)), HIGHEST),
         )
         d_projected[:, first : first + rank] = product(
-            d_before, step_weight[direction], ((1,), (1,)), HIGHEST
+            d_before, step_weight[2 * pair + direction], ((1,), (1,)), HIGHEST
         )
 
-    unit, inverse = normalise(load_interleaved(embedded))
-    gain = norm_gain[...]
-    normed = (unit * gain).astype(BF16)
     d_flat = d_projected[:, : 2 * group].astype(BF16)
     pack_halves(packed, firsts[1], product(d_flat, rounded, ((0,), (0,))))
-    d_all = product(d_flat, scan_weight[...], ((1,), (1,))) + d_values[...]
+    d_all = product(d_flat, pair_rows(scan_weight, pair, group)) + d_values[...]
     d_mixed = (d_all * sigma * (1.0 + mixed * (1.0 - sigma))).astype(BF16)
     pack_halves(packed, 0, product(normed, d_mixed, ((0,), (0,))))
-    d_normed = product(d_mixed, in_weight[...], ((1,), (1,)))
+    d_normed = product(d_mixed, in_weight[:, :inner], ((1,), (1,)))
     packed[firsts[4] : firsts[4] + 1] = jnp.sum(d_normed * unit, axis=0, keepdims=True)
     store_natural(d_embedded, normalise_pull(d_normed * gain, unit, inverse))
 
@@ -510,7 +550,7 @@
     natural = jnp.concatenate(
         [turned[pl.ds(row, edge, stride=edge), :] for row in range(edge)], axis=0
     )
-    gradient[...] = (own[...] + along_rows[...] + natural).astype(BF16)
+    gradient[...] = (own[...] + along_rows[...].reshape(own.shape) + natural).astype(BF16)
 
 
 def pack_kernel(gate, first, second, lines, blocks, stacked, *, shared):
@@ -579,7 +619,7 @@
             step_bias[index : index + 1] = joined(base + halves * (1 + direction), 1)
         gains = gains + whole[start + firsts[4] : start + firsts[4] + 1]
     norm_gain[...] = scale * gains
-    scan_weight[...] = jnp.concatenate(projected, axis=0).T
+    scan_weight[...] = jnp.concatenate(projected, axis=0)
 
 
 def shape_of(*sizes, dtype=F32):
@@ -623,54 +663,44 @@
     halves = inner // LANES
     scale = float(cells * lax.axis_size("row") * lax.axis_size("col")) ** (-0.5)
     gain = norm_gain.reshape(1, width)
-    value_weight, gate_weight = (in_weight[:, :inner], in_weight[:, inner:])
 
     embedded, turned = pl.pallas_call(
         functools.partial(embed_kernel, edge=edge),
         out_shape=(shape_of(cells, width), shape_of(cells, width)),
-        compiler_params=PARAMS,
+        compiler_params=SMALL,
         name="embed",
     )(classes.reshape(cells, 1), features.reshape(cells, width), table)
 
-    forward = pl.pallas_call(
-        functools.partial(forward_kernel, rank=rank, states=states),
-        out_shape=(
-            shape_of(cells, inner),
-            shape_of(cells, inner),
-            shape_of(2, cells, inner),
-            shape_of(cells, 2 * group),
-            shape_of(2, states, CHUNKS, inner),
-        ),
-        scratch_shapes=[
-            pltpu.VMEM((cells, inner), F32),
-            pltpu.VMEM((2, states, CHUNKS, inner), F32),
-            pltpu.VMEM((cells, inner), F32),
-            pltpu.VMEM((halves, cells, LANES), F32),
-            pltpu.VMEM((4 * states, cells, LANES), F32),
-        ],
-        compiler_params=PARAMS,
-        name="forward_scans",
-    )
-    axes = ("col", "row")
-    lines = [exchange(embedded, "col"), exchange(turned, "row")]
-    pairs = []
-    for pair in range(2):
-        two = slice(2 * pair, 2 * pair + 2)
-        weights = (
-            gain,
-            value_weight,
-            scan_weight[:, 2 * pair * group : 2 * (pair + 1) * group],
-            step_weight[two],
-            step_bias[two],
-            decay_log[two],
-        )
-        pairs.append((weights, skip_gain[two]))
-    kept, sums = ([], [])
-    for pair in range(2):
-        weights, skips = pairs[pair]
-        outputs = forward(lines[pair], *weights, skips)
-        kept.append(outputs[1:])
-        sums.append(exchange(outputs[0], axes[pair]))
+    weights = (gain, in_weight, scan_weight.T, step_weight, step_bias, decay_log, skip_gain)
+
+    def forward(pair, line):
+        return pl.pallas_call(
+            functools.partial(forward_kernel, pair=pair, rank=rank, states=states),
+            out_shape=(shape_of(cells, inner), shape_of(2, states, CHUNKS, inner)),
+            scratch_shapes=[
+                pltpu.VMEM((2, cells, inner), F32),
+                pltpu.VMEM((cells, inner), F32),
+                pltpu.VMEM((2, states, CHUNKS, inner), F32),
+                pltpu.VMEM((cells, inner), F32),
+                pltpu.VMEM((halves, cells, LANES), F32),
+                pltpu.VMEM((4 * states, cells, LANES), F32),
+            ],
+            compiler_params=MIDDLE,
+            cost_estimate=pl.CostEstimate(
+                flops=48 * 1024 * cells * inner,
+                bytes_accessed=8 * cells * inner,
+                transcendentals=4 * states * cells * inner,
+            ),
+            name="forward_scans",
+        )(line, *weights)
+
+    row_line, col_line = (exchange(embedded, "col"), exchange(turned, "row"))
+    row_sums, row_starts = forward(0, row_line)
+    row_sums, col_line = lax.optimization_barrier((row_sums, col_line))
+    along_rows = exchange(row_sums, "col")
+    col_sums, col_starts = forward(1, col_line)
+    along_rows, col_sums = lax.optimization_barrier((along_rows, col_sums))
+    along_cols = exchange(col_sums, "row")
 
     firsts = pack_sizes(inner, width, rank, states)
     gate_rows = halves * width + inner + 8
@@ -683,46 +713,53 @@
             shape_of(gate_rows, LANES),
         ),
         scratch_shapes=[pltpu.VMEM((halves, cells, LANES), F32)],
-        compiler_params=PARAMS,
+        compiler_params=SMALL,
         name="gate",
     )(
         embedded,
         gain,
-        gate_weight,
+        in_weight,
         output_gain.reshape(1, inner),
         output_weight,
         cotangent.reshape(cells, width),
-        sums[0],
-        sums[1],
+        along_rows,
+        along_cols,
     )
 
-    backward = pl.pallas_call(
-        functools.partial(backward_kernel, rank=rank, states=states),
-        out_shape=(shape_of(cells, width), shape_of(firsts[5], LANES)),
-        scratch_shapes=[
-            pltpu.VMEM((cells, inner), F32),
-            pltpu.VMEM((2, states, CHUNKS, inner), F32),
-            pltpu.VMEM((span + 1, states, CHUNKS, inner), F32),
-            pltpu.VMEM((span, states, CHUNKS, inner), F32),
-            pltpu.VMEM((cells, LANES), F32),
-            pltpu.VMEM((cells, inner), F32),
-            pltpu.VMEM((cells, inner), F32),
-            pltpu.VMEM((states, CHUNKS, inner), F32),
-            pltpu.VMEM((states, CHUNKS, inner), F32),
-            pltpu.VMEM((halves, cells, LANES), F32),
-            pltpu.VMEM((cells, inner), F32),
-            pltpu.VMEM((4 * states, cells, LANES), F32),
-            pltpu.VMEM((2 * states, cells, LANES), F32),
-        ],
-        compiler_params=PARAMS,
-        name="backward_scans",
-    )
-    arriving = [exchange(d_rows, "col"), exchange(d_cols, "row")]
-    outputs = []
-    for pair in range(2):
-        weights, skips = pairs[pair]
-        outputs.append(backward(lines[pair], *weights, *kept[pair], arriving[pair], skips))
-    returned = exchange(outputs[0][0], "col")
+    def backward(pair, line, starts, arriving):
+        return pl.pallas_call(
+            functools.partial(backward_kernel, pair=pair, rank=rank, states=states),
+            out_shape=(shape_of(cells, width), shape_of(firsts[5], LANES)),
+            scratch_shapes=[
+                pltpu.VMEM((2, cells, inner), F32),
+                pltpu.VMEM((cells, inner), F32),
+                pltpu.VMEM((2, states, CHUNKS, inner), F32),
+                pltpu.VMEM((span + 1, states, CHUNKS, inner), F32),
+                pltpu.VMEM((span, states, CHUNKS, inner), F32),
+                pltpu.VMEM((cells, LANES), F32),
+                pltpu.VMEM((cells, inner), F32),
+                pltpu.VMEM((cells, inner), F32),
+                pltpu.VMEM((states, CHUNKS, inner), F32),
+                pltpu.VMEM((states, CHUNKS, inner), F32),
+                pltpu.VMEM((halves, cells, LANES), F32),
+                pltpu.VMEM((cells, inner), F32),
+                pltpu.VMEM((4 * states, cells, LANES), F32),
+                pltpu.VMEM((2 * states, cells, LANES), F32),
+                pltpu.VMEM((2, cells, inner), F32),
+            ],
+            compiler_params=LARGE,
+            cost_estimate=pl.CostEstimate(
+                flops=96 * 1024 * cells * inner,
+                bytes_accessed=8 * cells * inner,
+                transcendentals=4 * states * cells * inner,
+            ),
+            name="backward_scans",
+        )(line, *weights, starts, arriving)
+
+    arriving_cols = exchange(d_cols, "row")
+    arriving_rows = exchange(d_rows, "col")
+    back_cols, packed_cols = backward(1, col_line, col_starts, arriving_cols)
+    back_rows, packed_rows = backward(0, row_line, row_starts, arriving_rows)
 
     row_count, col_count = (lax.axis_size("row"), lax.axis_size("col"))
     shared = firsts[1]
@@ -733,29 +770,29 @@
         functools.partial(pack_kernel, shared=shared),
         out_shape=shape_of(row_count, edge + share_rows, LANES),
         scratch_shapes=[pltpu.VMEM((stacked_rows, LANES), F32)],
-        compiler_params=PARAMS,
+        compiler_params=SMALL,
         name="pack",
-    )(gate_packed, outputs[0][1], outputs[1][1], outputs[1][0])
+    )(gate_packed, packed_rows, packed_cols, back_cols)
     received = lax.all_to_all(blocks, "row", 0, 0)
     partial = jnp.sum(received[:, edge:], axis=0)
-    partial = jnp.pad(partial, ((0, -share_rows % (col_count * 8)), (0, 0)))
-    partial = partial.reshape(col_count, -1, LANES)
-    owned = jnp.sum(lax.all_to_all(partial, "col", 0, 0), axis=0)
-    column_sums = share(owned, "col").reshape(-1, LANES)[:share_rows]
+    lines_back = back_rows.reshape(col_count, cells // col_count, width)
+    copies = jnp.broadcast_to(partial[None], (col_count,) + partial.shape)
+    crossed = lax.all_to_all(jnp.concatenate([lines_back, copies], axis=1), "col", 0, 0)
+    column_sums = jnp.sum(crossed[:, across:], axis=0)
     whole = share(column_sums, "row").reshape(stacked_rows, LANES)
 
     feature_grad = pl.pallas_call(
         functools.partial(finish_kernel, edge=edge),
         out_shape=shape_of(cells, width, dtype=BF16),
         scratch_shapes=[pltpu.VMEM((cells, width), F32)],
-        compiler_params=PARAMS,
+        compiler_params=SMALL,
         name="finish",
-    )(d_own, returned, received[:, :edge])
+    )(d_own, crossed[:, :across], received[:, :edge])
     grads = pl.pallas_call(
         functools.partial(unpack_kernel, scale=scale, rank=rank, states=states),
         out_shape=(
             shape_of(width, 2 * inner),
-            shape_of(inner, 4 * group),
+            shape_of(4 * group, inner),
             shape_of(4, rank, inner),
             shape_of(4, inner),
             shape_of(4, states, inner),
@@ -764,12 +801,14 @@
             shape_of(1, inner),
             shape_of(inner, width),
         ),
-        compiler_params=PARAMS,
+        compiler_params=SMALL,
         name="unpack",
     )(whole)
     return (
         feature_grad.reshape(edge, across, width),
-        *grads[:6],
+        grads[0],
+        grads[1].T,
+        *grads[2:6],
         grads[6].reshape(width),
         grads[7].reshape(inner),
         grads[8],

time: 235 us -> 186 us (0.79)
  Pallas kernels: 79.2 us -> 50.9 us
  starting transfers between devices: 38.5 us -> 22.5 us
  blocking collectives: 80.2 us -> 93.6 us
  waiting for transfers between devices: 24.1 us -> 14.1 us
  local copies, waits for them, and re-layouts: 11.4 us -> 3.15 us
    pallas_call x4, Pallas kernels: 74.2 us -> 46.7 us  [the longest x2 30 us: backward(): pl.pallas_call(functools.partial(backward_kernel, pair=pair, rank=rank, s...]
    all_to_all x5 -> x3, starting transfers between devices: 30.2 us -> 16.3 us  [exchange(): return lax.all_to_all(blocks, axis, 0, 0).reshape(length, width)]
    all_to_all x2 -> x3, blocking collectives: 33.6 us -> 45.4 us  [exchange(): return lax.all_to_all(blocks, axis, 0, 0).reshape(length, width)]
    all_to_all x5 -> x3, waiting for transfers between devices: 13.4 us -> 2.42 us  [exchange(): return lax.all_to_all(blocks, axis, 0, 0).reshape(length, width)]
    unnamed x47 -> x24, local copies, waits for them, and re-layouts: 9.56 us -> 1.33 us
    all_to_all x2 -> x1, blocking collectives: 29.5 us -> 31.1 us  [local(): lax.all_to_all(jnp.concatenate([lines_back, copies], axis=1), 'col', 0, 0)]
  transfers between devices with their start and end apart: 6 -> 4, of which waited for: 3 -> 2; matrix products, arithmetic and copies ran while one was open for 0% -> 0% of each run, Pallas kernels for 22% -> 18%
where the time goes in v1:
time: 186 us; the launch traced here: 185 us
  blocking collectives  93.6 us (50%)
  Pallas kernels  50.9 us (27%)
  starting transfers between devices  22.5 us (12%)
  waiting for transfers between devices  14.1 us (8%)
  local copies, waits for them, and re-layouts  3.15 us (2%)
    all_to_all x3, blocking collectives, exchange(): return lax.all_to_all(blocks, axis, 0, 0).reshape(length, width)  45.4 us
    all_to_all x1, blocking collectives, local(): lax.all_to_all(jnp.concatenate([lines_back, copies], axis=1), 'col', 0, 0)  31.1 us
    pallas_call x2, Pallas kernels, backward(): pl.pallas_call(functools.partial(backward_kernel, pair=pair, rank=rank, s...  30 us
    all_to_all x1, blocking collectives, local(): received = lax.all_to_all(blocks, 'row', 0, 0)  17.1 us
    pallas_call x2, Pallas kernels, forward(): pl.pallas_call(functools.partial(forward_kernel, pair=pair, rank=rank, st...  16.8 us
    all_to_all x3, starting transfers between devices, exchange(): return lax.all_to_all(blocks, axis, 0, 0).reshape(length, width)  16.3 us
    all_to_all x1, waiting for transfers between devices, share(): return lax.all_to_all(copies, axis, 0, 0)  11.6 us
    all_to_all x1, starting transfers between devices, share(): return lax.all_to_all(copies, axis, 0, 0)  6.29 us
  transfers between devices with their start and end apart: 4, of which 2 were waited for; matrix products, arithmetic and copies ran while one was open for 0% of the time, Pallas kernels for 18%

profile of v1, /device:TPU:1, one launch (start us, length us, event | category | flops | bytes accessed | tf_op | source)
XLA Modules:
  0.0 185.2 jit_solution(5776446069904974690)
XLA Ops:
  0.7 0.8 reshape.110.classes
  1.5 1.0 embed.1
  2.5 20.4 %all_to_all.45 = f32[16,16,128]{2,1,0:T(8,128)S(1)} all-to-all(f32[16,16,128]{2,1,0:T(8,128)S(1)} %bitcast.26), channel_id=1, replica_groups=mesh['row'=16,'col'=16] {'col'}, dimensions={0} | all-to-all | bytes 262144 | tf_op jit(solution)/shard_map/all_to_all | solution.py:633
  23.0 6.8 %all-to-all-start.1 = ((f32[16,16,128]{2,1,0:T(8,128)}), f32[16,16,128]{2,1,0:T(8,128)S(1)}, u32[]{:S(2)}, u32[]{:S(2)}) async-start(f32[16,16,128]{2,1,0:T(8,128)} %bitcast.7), calls=%async_computation.1 | async-start | bytes 262144 | tf_op jit(solution)/shard_map/all_to_all | solution.py:633
  29.8 0.6 copy-done.10
  30.4 8.7 %forward_scans.2 = (f32[256,256]{1,0:T(8,128)}, f32[2,16,8,256]{3,2,1,0:T(8,128)S(1)}) custom-call(f32[256,128]{1,0:T(8,128)S(1)} %bitcast.31, f32[1,128]{1,0:T(1,128)S(1)} %bitcast.39, bf16[128,512]{1,0:T(8,128)(2,1)S(1)} %copy-done, bf16[160,256]{1,0:T(8,128)(2,1)S(1)} %bitcast.44, f32[4,8,256]{2,1,0:T(8,128)S(1)} %copy-done.9, f32[4,256]{1,0:T(4,128)S(1)} %copy-done.10, ...), custom_call_target="tpu_custom_call" | custom-call | flops 3221225472 | bytes 524288 | tf_op jit(solution)/shard_map/forward_scans/pallas_call | solution.py:677
  39.1 3.6 %all-to-all-start.2 = ((f32[16,16,256]{2,1,0:T(8,128)}), f32[16,16,256]{2,1,0:T(8,128)S(1)}, u32[]{:S(2)}, u32[]{:S(2)}) async-start(f32[16,16,256]{2,1,0:T(8,128)} %bitcast.9), calls=%async_computation.2 | async-start | bytes 524288 | tf_op jit(solution)/shard_map/all_to_all | solution.py:633
  42.8 8.0 %forward_scans.3 = (f32[256,256]{1,0:T(8,128)S(1)}, f32[2,16,8,256]{3,2,1,0:T(8,128)S(1)}) custom-call(f32[256,128]{1,0:T(8,128)S(1)} %bitcast.33, f32[1,128]{1,0:T(1,128)S(1)} %bitcast.40, bf16[128,512]{1,0:T(8,128)(2,1)S(1)} %copy-done, bf16[160,256]{1,0:T(8,128)(2,1)S(1)} %bitcast.45, f32[4,8,256]{2,1,0:T(8,128)S(1)} %copy-done.9, ...), custom_call_target="tpu_custom_call" | custom-call | flops 3221225472 | bytes 524288 | tf_op jit(solution)/shard_map/forward_scans/pallas_call | solution.py:677
  50.8 2.4 %all-to-all-done.2 = f32[16,16,256]{2,1,0:T(8,128)S(1)} async-done(((f32[16,16,256]{2,1,0:T(8,128)}), f32[16,16,256]{2,1,0:T(8,128)S(1)}, u32[]{:S(2)}, u32[]{:S(2)}) %all-to-all-start.2) | async-done | bytes 262176 | tf_op jit(solution)/shard_map/all_to_all | solution.py:633
  53.2 14.4 %all_to_all.46 = f32[16,16,256]{2,1,0:T(8,128)S(1)} all-to-all(f32[16,16,256]{2,1,0:T(8,128)S(1)} %bitcast.29), channel_id=1, replica_groups=mesh['row'=16,'col'=16] {'row'}, dimensions={0} | all-to-all | bytes 524288 | tf_op jit(solution)/shard_map/all_to_all | solution.py:633
  67.6 0.7 copy-done.5
  68.3 1.5 gate.1
  69.8 10.6 %all_to_all.47 = f32[16,16,256]{2,1,0:T(8,128)S(1)} all-to-all(f32[16,16,256]{2,1,0:T(8,128)S(1)} %bitcast.30), channel_id=1, replica_groups=mesh['row'=16,'col'=16] {'row'}, dimensions={0} | all-to-all | bytes 524288 | tf_op jit(solution)/shard_map/all_to_all | solution.py:633
  80.4 5.9 %all-to-all-start.4 = ((f32[16,16,256]{2,1,0:T(8,128)}), f32[16,16,256]{2,1,0:T(8,128)S(1)}, u32[]{:S(2)}, u32[]{:S(2)}) async-start(f32[16,16,256]{2,1,0:T(8,128)} %bitcast.13), calls=%async_computation.4 | async-start | bytes 524288 | tf_op jit(solution)/shard_map/all_to_all | solution.py:633
  86.3 15.0 %backward_scans.3 = (f32[256,128]{1,0:T(8,128)S(1)}, f32[520,128]{1,0:T(8,128)S(1)}) custom-call(f32[256,128]{1,0:T(8,128)S(1)} %bitcast.34, f32[1,128]{1,0:T(1,128)S(1)} %bitcast.42, bf16[128,512]{1,0:T(8,128)(2,1)S(1)} %copy-done, bf16[160,256]{1,0:T(8,128)(2,1)S(1)} %bitcast.46, f32[4,8,256]{2,1,0:T(8,128)S(1)} %copy-done.9, f32[4,256]{1,0:T(4,128)S(1)} %copy-done.10, ...), custom_call_target="tpu_custom_call" | custom-call | flops 6442450944 | bytes 524288 | tf_op jit(solution)/shard_map/backward_scans/pallas_call | solution.py:730
  101.3 15.0 %backward_scans.2 = (f32[256,128]{1,0:T(8,128)S(1)}, f32[520,128]{1,0:T(8,128)S(1)}) custom-call(f32[256,128]{1,0:T(8,128)S(1)} %bitcast.32, f32[1,128]{1,0:T(1,128)S(1)} %bitcast.43, bf16[128,512]{1,0:T(8,128)(2,1)S(1)} %copy-done, bf16[160,256]{1,0:T(8,128)(2,1)S(1)} %bitcast.47, f32[4,8,256]{2,1,0:T(8,128)S(1)} %copy-done.9, f32[4,256]{1,0:T(4,128)S(1)} %copy-done.10, ...), custom_call_target="tpu_custom_call" | custom-call | flops 6442450944 | bytes 524288 | tf_op jit(solution)/shard_map/backward_scans/pallas_call | solution.py:730
  116.3 0.1 pack.1
  116.3 17.1 %all_to_all.48 = f32[16,104,128]{2,1,0:T(8,128)S(1)} all-to-all(f32[16,104,128]{2,1,0:T(8,128)S(1)} %pack.1), channel_id=1, replica_groups=mesh['row'=16,'col'=16] {'row'}, dimensions={0} | all-to-all | bytes 1703936 | tf_op jit(solution)/shard_map/all_to_all | solution.py:776
  133.6 31.1 %all_to_all.49 = f32[16,104,128]{2,1,0:T(8,128)S(1)} all-to-all(f32[16,104,128]{2,1,0:T(8,128)S(1)} %pad_maximum_fusion), channel_id=1, replica_groups=mesh['row'=16,'col'=16] {'col'}, dimensions={0} | all-to-all | bytes 1703936 | tf_op jit(solution)/shard_map/all_to_all | solution.py:780
  164.8 0.9 broadcast_in_dim.5
  165.7 6.3 %all-to-all-start.8 = ((f32[16,88,128]{2,1,0:T(8,128)}), f32[16,88,128]{2,1,0:T(8,128)S(1)}, u32[]{:S(2)}, u32[]{:S(2)}) async-start(f32[16,88,128]{2,1,0:T(8,128)} %broadcast_in_dim.5), calls=%async_computation.8 | async-start | bytes 1441792 | tf_op jit(solution)/shard_map/all_to_all | solution.py:639
  172.0 0.7 finish.1
  172.7 11.6 %all-to-all-done.8 = f32[16,88,128]{2,1,0:T(8,128)S(1)} async-done(((f32[16,88,128]{2,1,0:T(8,128)}), f32[16,88,128]{2,1,0:T(8,128)S(1)}, u32[]{:S(2)}, u32[]{:S(2)}) %all-to-all-start.8) | async-done | bytes 720928 | tf_op jit(solution)/shard_map/all_to_all | solution.py:639
  184.3 0.9 unpack.1
  (30 shorter events, 0.3 us)
Async XLA Ops:
  0.6 0.9 copy-start.4
  0.7 0.9 copy-start.1
  2.5 27.2 %copy-start.8 = (f32[4,16,256]{2,1,0:T(8,128)S(1)}, f32[4,16,256]{2,1,0:T(8,128)}, u32[]{:S(2)}) copy-start(f32[4,16,256]{2,1,0:T(8,128)} %decay_log.7) | copy-start | bytes 196612
  22.9 6.8 %copy-start = (bf16[128,512]{1,0:T(8,128)(2,1)S(1)}, bf16[128,512]{1,0:T(8,128)(2,1)}, u32[]{:S(2)}) copy-start(bf16[128,512]{1,0:T(8,128)(2,1)} %in_weight.9) | copy-start | bytes 393220
  22.9 6.8 %copy-start.7 = (bf16[256,160]{0,1:T(8,128)(2,1)S(1)}, bf16[256,160]{0,1:T(8,128)(2,1)}, u32[]{:S(2)}) copy-start(bf16[256,160]{0,1:T(8,128)(2,1)} %param.19) | copy-start | bytes 245764
  22.9 6.8 %copy-start.9 = (f32[4,8,256]{2,1,0:T(8,128)S(1)}, f32[4,8,256]{2,1,0:T(8,128)}, u32[]{:S(2)}) copy-start(f32[4,8,256]{2,1,0:T(8,128)} %step_weight.7) | copy-start | bytes 98308
  22.9 6.8 %copy-start.11 = (f32[4,256]{1,0:T(4,128)S(1)}, f32[4,256]{1,0:T(4,128)}, u32[]{:S(2)}) copy-start(f32[4,256]{1,0:T(4,128)} %skip_gain.7) | copy-start | bytes 12292
  23.0 16.2 %all-to-all-start.1 = ((f32[16,16,128]{2,1,0:T(8,128)}), f32[16,16,128]{2,1,0:T(8,128)S(1)}, u32[]{:S(2)}, u32[]{:S(2)}) async-start(f32[16,16,128]{2,1,0:T(8,128)} %bitcast.7), calls=%async_computation.1 | async-start | bytes 262144 | tf_op jit(solution)/shard_map/all_to_all | solution.py:633
  29.7 0.7 copy-start.10
  29.7 0.7 copy-start.6
  39.1 14.1 %all-to-all-start.2 = ((f32[16,16,256]{2,1,0:T(8,128)}), f32[16,16,256]{2,1,0:T(8,128)S(1)}, u32[]{:S(2)}, u32[]{:S(2)}) async-start(f32[16,16,256]{2,1,0:T(8,128)} %bitcast.9), calls=%async_computation.2 | async-start | bytes 524288 | tf_op jit(solution)/shard_map/all_to_all | solution.py:633
  53.2 14.4 %copy-start.2 = (bf16[256,128]{1,0:T(8,128)(2,1)S(1)}, bf16[256,128]{1,0:T(8,128)(2,1)}, u32[]{:S(2)}) copy-start(bf16[256,128]{1,0:T(8,128)(2,1)} %output_weight.1) | copy-start | bytes 196612
  53.2 14.4 %copy-start.3 = (bf16[16,16,128]{2,1,0:T(8,128)(2,1)S(1)}, bf16[16,16,128]{2,1,0:T(8,128)(2,1)}, u32[]{:S(2)}) copy-start(bf16[16,16,128]{2,1,0:T(8,128)(2,1)} %param.15) | copy-start | bytes 196612
  67.6 0.7 copy-start.5
  80.4 20.9 %all-to-all-start.4 = ((f32[16,16,256]{2,1,0:T(8,128)}), f32[16,16,256]{2,1,0:T(8,128)S(1)}, u32[]{:S(2)}, u32[]{:S(2)}) async-start(f32[16,16,256]{2,1,0:T(8,128)} %bitcast.13), calls=%async_computation.4 | async-start | bytes 524288 | tf_op jit(solution)/shard_map/all_to_all | solution.py:633
  165.7 18.7 %all-to-all-start.8 = ((f32[16,88,128]{2,1,0:T(8,128)}), f32[16,88,128]{2,1,0:T(8,128)S(1)}, u32[]{:S(2)}, u32[]{:S(2)}) async-start(f32[16,88,128]{2,1,0:T(8,128)} %broadcast_in_dim.5), calls=%async_computation.8 | async-start | bytes 1441792 | tf_op jit(solution)/shard_map/all_to_all | solution.py:639

commit v2 on v1

--- a/solution.py
+++ b/solution.py
@@ -130,7 +130,7 @@
             columns[direction * wanted + 2 * pair + 1] = wide[:, LANES:]
             return unused
 
-        sweep(wanted // 2, one, 0, 8)
+        sweep(wanted // 2, one, 0, 16)
 
 
 def sum_columns(terms, target, first):
@@ -144,7 +144,7 @@
         target[...] = jnp.where(place == first // 2 + pair, product(both, copies), target[...])
         return unused
 
-    sweep(terms.shape[0] // 2, one, 0, 4)
+    sweep(terms.shape[0] // 2, one, 0, 16)
 
 
 def slot(place):
@@ -512,7 +512,7 @@
             d_steps[at, :] = value * d_drive + LN2 * d_step
             return tuple(after)
 
-        sweep(span, pull, tuple(enter[n] for n in range(states)), 2)
+        sweep(span, pull, tuple(enter[n] for n in range(states)), 4)
         first = direction * group
         sum_columns(terms, d_projected, first + rank)
         pack_halves(

time: 186 us -> 181 us (0.973)
  Pallas kernels: 50.9 us -> 45.5 us
    pallas_call x2, Pallas kernels: 30 us -> 26.1 us  [backward(): pl.pallas_call(functools.partial(backward_kernel, pair=pair, rank=rank, s...]
  transfers between devices with their start and end apart: 4 -> 4, of which waited for: 2 -> 2; matrix products, arithmetic and copies ran while one was open for 0% -> 0% of each run, Pallas kernels for 18% -> 16%
where the time goes in v2:
time: 181 us; the launch traced here: 180 us
  blocking collectives  93.6 us (52%)
  Pallas kernels  45.5 us (25%)
  starting transfers between devices  21.8 us (12%)
  waiting for transfers between devices  14.8 us (8%)
  local copies, waits for them, and re-layouts  3.15 us (2%)
    all_to_all x3, blocking collectives, exchange(): return lax.all_to_all(blocks, axis, 0, 0).reshape(length, width)  45.4 us
    all_to_all x1, blocking collectives, local(): lax.all_to_all(jnp.concatenate([lines_back, copies], axis=1), 'col', 0, 0)  31.1 us
    pallas_call x2, Pallas kernels, backward(): pl.pallas_call(functools.partial(backward_kernel, pair=pair, rank=rank, s...  26.1 us
    all_to_all x1, blocking collectives, local(): received = lax.all_to_all(blocks, 'row', 0, 0)  17.1 us
    all_to_all x3, starting transfers between devices, exchange(): return lax.all_to_all(blocks, axis, 0, 0).reshape(length, width)  15.5 us
    pallas_call x2, Pallas kernels, forward(): pl.pallas_call(functools.partial(forward_kernel, pair=pair, rank=rank, st...  15.3 us
    all_to_all x1, waiting for transfers between devices, share(): return lax.all_to_all(copies, axis, 0, 0)  11.6 us
    all_to_all x1, starting transfers between devices, share(): return lax.all_to_all(copies, axis, 0, 0)  6.29 us
  transfers between devices with their start and end apart: 4, of which 2 were waited for; matrix products, arithmetic and copies ran while one was open for 0% of the time, Pallas kernels for 16%

profile of v2, /device:TPU:1, one launch (start us, length us, event | category | flops | bytes accessed | tf_op | source)
XLA Modules:
  0.0 179.9 jit_solution(785364223974020188)
XLA Ops:
  0.7 0.8 reshape.110.classes
  1.5 1.0 embed.1
  2.5 20.4 %all_to_all.45 = f32[16,16,128]{2,1,0:T(8,128)S(1)} all-to-all(f32[16,16,128]{2,1,0:T(8,128)S(1)} %bitcast.26), channel_id=1, replica_groups=mesh['row'=16,'col'=16] {'col'}, dimensions={0} | all-to-all | bytes 262144 | tf_op jit(solution)/shard_map/all_to_all | solution.py:633
  23.0 6.8 %all-to-all-start.1 = ((f32[16,16,128]{2,1,0:T(8,128)}), f32[16,16,128]{2,1,0:T(8,128)S(1)}, u32[]{:S(2)}, u32[]{:S(2)}) async-start(f32[16,16,128]{2,1,0:T(8,128)} %bitcast.7), calls=%async_computation.1 | async-start | bytes 262144 | tf_op jit(solution)/shard_map/all_to_all | solution.py:633
  29.8 0.6 copy-done.10
  30.4 8.0 %forward_scans.2 = (f32[256,256]{1,0:T(8,128)}, f32[2,16,8,256]{3,2,1,0:T(8,128)S(1)}) custom-call(f32[256,128]{1,0:T(8,128)S(1)} %bitcast.31, f32[1,128]{1,0:T(1,128)S(1)} %bitcast.39, bf16[128,512]{1,0:T(8,128)(2,1)S(1)} %copy-done, bf16[160,256]{1,0:T(8,128)(2,1)S(1)} %bitcast.44, f32[4,8,256]{2,1,0:T(8,128)S(1)} %copy-done.9, f32[4,256]{1,0:T(4,128)S(1)} %copy-done.10, ...), custom_call_target="tpu_custom_call" | custom-call | flops 3221225472 | bytes 524288 | tf_op jit(solution)/shard_map/forward_scans/pallas_call | solution.py:677
  38.4 3.6 %all-to-all-start.2 = ((f32[16,16,256]{2,1,0:T(8,128)}), f32[16,16,256]{2,1,0:T(8,128)S(1)}, u32[]{:S(2)}, u32[]{:S(2)}) async-start(f32[16,16,256]{2,1,0:T(8,128)} %bitcast.9), calls=%async_computation.2 | async-start | bytes 524288 | tf_op jit(solution)/shard_map/all_to_all | solution.py:633
  42.0 7.3 %forward_scans.3 = (f32[256,256]{1,0:T(8,128)S(1)}, f32[2,16,8,256]{3,2,1,0:T(8,128)S(1)}) custom-call(f32[256,128]{1,0:T(8,128)S(1)} %bitcast.33, f32[1,128]{1,0:T(1,128)S(1)} %bitcast.40, bf16[128,512]{1,0:T(8,128)(2,1)S(1)} %copy-done, bf16[160,256]{1,0:T(8,128)(2,1)S(1)} %bitcast.45, f32[4,8,256]{2,1,0:T(8,128)S(1)} %copy-done.9, ...), custom_call_target="tpu_custom_call" | custom-call | flops 3221225472 | bytes 524288 | tf_op jit(solution)/shard_map/forward_scans/pallas_call | solution.py:677
  49.3 3.1 %all-to-all-done.2 = f32[16,16,256]{2,1,0:T(8,128)S(1)} async-done(((f32[16,16,256]{2,1,0:T(8,128)}), f32[16,16,256]{2,1,0:T(8,128)S(1)}, u32[]{:S(2)}, u32[]{:S(2)}) %all-to-all-start.2) | async-done | bytes 262176 | tf_op jit(solution)/shard_map/all_to_all | solution.py:633
  52.5 14.4 %all_to_all.46 = f32[16,16,256]{2,1,0:T(8,128)S(1)} all-to-all(f32[16,16,256]{2,1,0:T(8,128)S(1)} %bitcast.29), channel_id=1, replica_groups=mesh['row'=16,'col'=16] {'row'}, dimensions={0} | all-to-all | bytes 524288 | tf_op jit(solution)/shard_map/all_to_all | solution.py:633
  66.9 0.7 copy-done.5
  67.5 1.5 gate.1
  69.0 10.6 %all_to_all.47 = f32[16,16,256]{2,1,0:T(8,128)S(1)} all-to-all(f32[16,16,256]{2,1,0:T(8,128)S(1)} %bitcast.30), channel_id=1, replica_groups=mesh['row'=16,'col'=16] {'row'}, dimensions={0} | all-to-all | bytes 524288 | tf_op jit(solution)/shard_map/all_to_all | solution.py:633
  79.6 5.1 %all-to-all-start.4 = ((f32[16,16,256]{2,1,0:T(8,128)}), f32[16,16,256]{2,1,0:T(8,128)S(1)}, u32[]{:S(2)}, u32[]{:S(2)}) async-start(f32[16,16,256]{2,1,0:T(8,128)} %bitcast.13), calls=%async_computation.4 | async-start | bytes 524288 | tf_op jit(solution)/shard_map/all_to_all | solution.py:633
  84.8 13.0 %backward_scans.3 = (f32[256,128]{1,0:T(8,128)S(1)}, f32[520,128]{1,0:T(8,128)S(1)}) custom-call(f32[256,128]{1,0:T(8,128)S(1)} %bitcast.34, f32[1,128]{1,0:T(1,128)S(1)} %bitcast.42, bf16[128,512]{1,0:T(8,128)(2,1)S(1)} %copy-done, bf16[160,256]{1,0:T(8,128)(2,1)S(1)} %bitcast.46, f32[4,8,256]{2,1,0:T(8,128)S(1)} %copy-done.9, f32[4,256]{1,0:T(4,128)S(1)} %copy-done.10, ...), custom_call_target="tpu_custom_call" | custom-call | flops 6442450944 | bytes 524288 | tf_op jit(solution)/shard_map/backward_scans/pallas_call | solution.py:730
  97.8 13.1 %backward_scans.2 = (f32[256,128]{1,0:T(8,128)S(1)}, f32[520,128]{1,0:T(8,128)S(1)}) custom-call(f32[256,128]{1,0:T(8,128)S(1)} %bitcast.32, f32[1,128]{1,0:T(1,128)S(1)} %bitcast.43, bf16[128,512]{1,0:T(8,128)(2,1)S(1)} %copy-done, bf16[160,256]{1,0:T(8,128)(2,1)S(1)} %bitcast.47, f32[4,8,256]{2,1,0:T(8,128)S(1)} %copy-done.9, f32[4,256]{1,0:T(4,128)S(1)} %copy-done.10, ...), custom_call_target="tpu_custom_call" | custom-call | flops 6442450944 | bytes 524288 | tf_op jit(solution)/shard_map/backward_scans/pallas_call | solution.py:730
  110.9 0.1 pack.1
  111.0 17.1 %all_to_all.48 = f32[16,104,128]{2,1,0:T(8,128)S(1)} all-to-all(f32[16,104,128]{2,1,0:T(8,128)S(1)} %pack.1), channel_id=1, replica_groups=mesh['row'=16,'col'=16] {'row'}, dimensions={0} | all-to-all | bytes 1703936 | tf_op jit(solution)/shard_map/all_to_all | solution.py:776
  128.3 31.1 %all_to_all.49 = f32[16,104,128]{2,1,0:T(8,128)S(1)} all-to-all(f32[16,104,128]{2,1,0:T(8,128)S(1)} %pad_maximum_fusion), channel_id=1, replica_groups=mesh['row'=16,'col'=16] {'col'}, dimensions={0} | all-to-all | bytes 1703936 | tf_op jit(solution)/shard_map/all_to_all | solution.py:780
  159.4 0.9 broadcast_in_dim.5
  160.3 6.3 %all-to-all-start.8 = ((f32[16,88,128]{2,1,0:T(8,128)}), f32[16,88,128]{2,1,0:T(8,128)S(1)}, u32[]{:S(2)}, u32[]{:S(2)}) async-start(f32[16,88,128]{2,1,0:T(8,128)} %broadcast_in_dim.5), calls=%async_computation.8 | async-start | bytes 1441792 | tf_op jit(solution)/shard_map/all_to_all | solution.py:639
  166.7 0.7 finish.1
  167.4 11.6 %all-to-all-done.8 = f32[16,88,128]{2,1,0:T(8,128)S(1)} async-done(((f32[16,88,128]{2,1,0:T(8,128)}), f32[16,88,128]{2,1,0:T(8,128)S(1)}, u32[]{:S(2)}, u32[]{:S(2)}) %all-to-all-start.8) | async-done | bytes 720928 | tf_op jit(solution)/shard_map/all_to_all | solution.py:639
  179.0 0.9 unpack.1
  (30 shorter events, 0.3 us)
Async XLA Ops:
  0.6 0.9 copy-start.4
  0.7 0.9 copy-start.1
  2.5 27.2 %copy-start.8 = (f32[4,16,256]{2,1,0:T(8,128)S(1)}, f32[4,16,256]{2,1,0:T(8,128)}, u32[]{:S(2)}) copy-start(f32[4,16,256]{2,1,0:T(8,128)} %decay_log.7) | copy-start | bytes 196612
  22.9 6.8 %copy-start = (bf16[128,512]{1,0:T(8,128)(2,1)S(1)}, bf16[128,512]{1,0:T(8,128)(2,1)}, u32[]{:S(2)}) copy-start(bf16[128,512]{1,0:T(8,128)(2,1)} %in_weight.9) | copy-start | bytes 393220
  22.9 6.8 %copy-start.7 = (bf16[256,160]{0,1:T(8,128)(2,1)S(1)}, bf16[256,160]{0,1:T(8,128)(2,1)}, u32[]{:S(2)}) copy-start(bf16[256,160]{0,1:T(8,128)(2,1)} %param.19) | copy-start | bytes 245764
  22.9 6.8 %copy-start.9 = (f32[4,8,256]{2,1,0:T(8,128)S(1)}, f32[4,8,256]{2,1,0:T(8,128)}, u32[]{:S(2)}) copy-start(f32[4,8,256]{2,1,0:T(8,128)} %step_weight.7) | copy-start | bytes 98308
  22.9 6.8 %copy-start.11 = (f32[4,256]{1,0:T(4,128)S(1)}, f32[4,256]{1,0:T(4,128)}, u32[]{:S(2)}) copy-start(f32[4,256]{1,0:T(4,128)} %skip_gain.7) | copy-start | bytes 12292
  23.0 15.4 %all-to-all-start.1 = ((f32[16,16,128]{2,1,0:T(8,128)}), f32[16,16,128]{2,1,0:T(8,128)S(1)}, u32[]{:S(2)}, u32[]{:S(2)}) async-start(f32[16,16,128]{2,1,0:T(8,128)} %bitcast.7), calls=%async_computation.1 | async-start | bytes 262144 | tf_op jit(solution)/shard_map/all_to_all | solution.py:633
  29.7 0.7 copy-start.10
  29.7 0.7 copy-start.6
  38.4 14.1 %all-to-all-start.2 = ((f32[16,16,256]{2,1,0:T(8,128)}), f32[16,16,256]{2,1,0:T(8,128)S(1)}, u32[]{:S(2)}, u32[]{:S(2)}) async-start(f32[16,16,256]{2,1,0:T(8,128)} %bitcast.9), calls=%async_computation.2 | async-start | bytes 524288 | tf_op jit(solution)/shard_map/all_to_all | solution.py:633
  52.5 14.4 %copy-start.2 = (bf16[256,128]{1,0:T(8,128)(2,1)S(1)}, bf16[256,128]{1,0:T(8,128)(2,1)}, u32[]{:S(2)}) copy-start(bf16[256,128]{1,0:T(8,128)(2,1)} %output_weight.1) | copy-start | bytes 196612
  52.5 14.4 %copy-start.3 = (bf16[16,16,128]{2,1,0:T(8,128)(2,1)S(1)}, bf16[16,16,128]{2,1,0:T(8,128)(2,1)}, u32[]{:S(2)}) copy-start(bf16[16,16,128]{2,1,0:T(8,128)(2,1)} %param.15) | copy-start | bytes 196612
  66.8 0.7 copy-start.5
  79.6 18.2 %all-to-all-start.4 = ((f32[16,16,256]{2,1,0:T(8,128)}), f32[16,16,256]{2,1,0:T(8,128)S(1)}, u32[]{:S(2)}, u32[]{:S(2)}) async-start(f32[16,16,256]{2,1,0:T(8,128)} %bitcast.13), calls=%async_computation.4 | async-start | bytes 524288 | tf_op jit(solution)/shard_map/all_to_all | solution.py:633
  160.3 18.7 %all-to-all-start.8 = ((f32[16,88,128]{2,1,0:T(8,128)}), f32[16,88,128]{2,1,0:T(8,128)S(1)}, u32[]{:S(2)}, u32[]{:S(2)}) async-start(f32[16,88,128]{2,1,0:T(8,128)} %broadcast_in_dim.5), calls=%async_computation.8 | async-start | bytes 1441792 | tf_op jit(solution)/shard_map/all_to_all | solution.py:639

commit v3 on v2

--- a/solution.py
+++ b/solution.py
@@ -463,7 +463,7 @@
             begin = tuple(starts[direction, n, :, lanes] for n in range(states))
             for n in range(states):
                 history[0, n, :, lanes] = begin[n]
-            unused, total = sweep(span, advance, (begin, zero), 4)
+            unused, total = sweep(span, advance, (begin, zero), 8)
 
             def retreat(turn, carried, lanes=lanes, rows=rows, probe=probe):
                 back = span - 1 - turn
@@ -475,7 +475,7 @@
                     for n in range(states)
                 )
 
-            carried = sweep(span, retreat, (zero,) * states, 8)
+            carried = sweep(span, retreat, (zero,) * states, 16)
             for n in range(states):
                 factor = jnp.exp2(total * rates[direction, n, :, lanes])
                 enter[n, :, lanes] = chain_chunks(factor, carried[n], direction == 1)
@@ -532,7 +532,7 @@
             product(lowranks[direction], d_before, ((0,), (0,)), HIGHEST),
         )
         d_projected[:, first : first + rank] = product(
-            d_before, step_weight[2 * pair + direction], ((1,), (1,)), HIGHEST
+            d_before, step_weight[2 * pair + direction], ((1,), (1,))
         )
 
     d_flat = d_projected[:, : 2 * group].astype(BF16)

time: 181 us -> 179 us (0.989)
    pallas_call x2, Pallas kernels: 26.1 us -> 24.3 us  [backward(): pl.pallas_call(functools.partial(backward_kernel, pair=pair, rank=rank, s...]
where the time goes in v3:
time: 179 us; the launch traced here: 178 us
  blocking collectives  93.6 us (52%)
  Pallas kernels  43.7 us (24%)
  starting transfers between devices  21.8 us (12%)
  waiting for transfers between devices  14.8 us (8%)
  local copies, waits for them, and re-layouts  3.15 us (2%)
    all_to_all x3, blocking collectives, exchange(): return lax.all_to_all(blocks, axis, 0, 0).reshape(length, width)  45.4 us
    all_to_all x1, blocking collectives, local(): lax.all_to_all(jnp.concatenate([lines_back, copies], axis=1), 'col', 0, 0)  31.1 us
    pallas_call x2, Pallas kernels, backward(): pl.pallas_call(functools.partial(backward_kernel, pair=pair, rank=rank, s...  24.3 us
    all_to_all x1, blocking collectives, local(): received = lax.all_to_all(blocks, 'row', 0, 0)  17.1 us
    all_to_all x3, starting transfers between devices, exchange(): return lax.all_to_all(blocks, axis, 0, 0).reshape(length, width)  15.5 us
    pallas_call x2, Pallas kernels, forward(): pl.pallas_call(functools.partial(forward_kernel, pair=pair, rank=rank, st...  15.3 us
    all_to_all x1, waiting for transfers between devices, share(): return lax.all_to_all(copies, axis, 0, 0)  11.6 us
    all_to_all x1, starting transfers between devices, share(): return lax.all_to_all(copies, axis, 0, 0)  6.29 us
  transfers between devices with their start and end apart: 4, of which 2 were waited for; matrix products, arithmetic and copies ran while one was open for 0% of the time, Pallas kernels for 16%

profile of v3, /device:TPU:1, one launch (start us, length us, event | category | flops | bytes accessed | tf_op | source)
XLA Modules:
  0.0 178.1 jit_solution(11777874004309652443)
XLA Ops:
  0.7 0.8 reshape.110.classes
  1.5 1.0 embed.1
  2.5 20.4 %all_to_all.45 = f32[16,16,128]{2,1,0:T(8,128)S(1)} all-to-all(f32[16,16,128]{2,1,0:T(8,128)S(1)} %bitcast.26), channel_id=1, replica_groups=mesh['row'=16,'col'=16] {'col'}, dimensions={0} | all-to-all | bytes 262144 | tf_op jit(solution)/shard_map/all_to_all | solution.py:633
  23.0 6.8 %all-to-all-start.1 = ((f32[16,16,128]{2,1,0:T(8,128)}), f32[16,16,128]{2,1,0:T(8,128)S(1)}, u32[]{:S(2)}, u32[]{:S(2)}) async-start(f32[16,16,128]{2,1,0:T(8,128)} %bitcast.7), calls=%async_computation.1 | async-start | bytes 262144 | tf_op jit(solution)/shard_map/all_to_all | solution.py:633
  29.8 0.6 copy-done.10
  30.4 8.0 %forward_scans.2 = (f32[256,256]{1,0:T(8,128)}, f32[2,16,8,256]{3,2,1,0:T(8,128)S(1)}) custom-call(f32[256,128]{1,0:T(8,128)S(1)} %bitcast.31, f32[1,128]{1,0:T(1,128)S(1)} %bitcast.39, bf16[128,512]{1,0:T(8,128)(2,1)S(1)} %copy-done, bf16[160,256]{1,0:T(8,128)(2,1)S(1)} %bitcast.44, f32[4,8,256]{2,1,0:T(8,128)S(1)} %copy-done.9, f32[4,256]{1,0:T(4,128)S(1)} %copy-done.10, ...), custom_call_target="tpu_custom_call" | custom-call | flops 3221225472 | bytes 524288 | tf_op jit(solution)/shard_map/forward_scans/pallas_call | solution.py:677
  38.4 3.6 %all-to-all-start.2 = ((f32[16,16,256]{2,1,0:T(8,128)}), f32[16,16,256]{2,1,0:T(8,128)S(1)}, u32[]{:S(2)}, u32[]{:S(2)}) async-start(f32[16,16,256]{2,1,0:T(8,128)} %bitcast.9), calls=%async_computation.2 | async-start | bytes 524288 | tf_op jit(solution)/shard_map/all_to_all | solution.py:633
  42.0 7.3 %forward_scans.3 = (f32[256,256]{1,0:T(8,128)S(1)}, f32[2,16,8,256]{3,2,1,0:T(8,128)S(1)}) custom-call(f32[256,128]{1,0:T(8,128)S(1)} %bitcast.33, f32[1,128]{1,0:T(1,128)S(1)} %bitcast.40, bf16[128,512]{1,0:T(8,128)(2,1)S(1)} %copy-done, bf16[160,256]{1,0:T(8,128)(2,1)S(1)} %bitcast.45, f32[4,8,256]{2,1,0:T(8,128)S(1)} %copy-done.9, ...), custom_call_target="tpu_custom_call" | custom-call | flops 3221225472 | bytes 524288 | tf_op jit(solution)/shard_map/forward_scans/pallas_call | solution.py:677
  49.3 3.1 %all-to-all-done.2 = f32[16,16,256]{2,1,0:T(8,128)S(1)} async-done(((f32[16,16,256]{2,1,0:T(8,128)}), f32[16,16,256]{2,1,0:T(8,128)S(1)}, u32[]{:S(2)}, u32[]{:S(2)}) %all-to-all-start.2) | async-done | bytes 262176 | tf_op jit(solution)/shard_map/all_to_all | solution.py:633
  52.5 14.4 %all_to_all.46 = f32[16,16,256]{2,1,0:T(8,128)S(1)} all-to-all(f32[16,16,256]{2,1,0:T(8,128)S(1)} %bitcast.29), channel_id=1, replica_groups=mesh['row'=16,'col'=16] {'row'}, dimensions={0} | all-to-all | bytes 524288 | tf_op jit(solution)/shard_map/all_to_all | solution.py:633
  66.9 0.7 copy-done.5
  67.5 1.5 gate.1
  69.0 10.6 %all_to_all.47 = f32[16,16,256]{2,1,0:T(8,128)S(1)} all-to-all(f32[16,16,256]{2,1,0:T(8,128)S(1)} %bitcast.30), channel_id=1, replica_groups=mesh['row'=16,'col'=16] {'row'}, dimensions={0} | all-to-all | bytes 524288 | tf_op jit(solution)/shard_map/all_to_all | solution.py:633
  79.6 5.1 %all-to-all-start.4 = ((f32[16,16,256]{2,1,0:T(8,128)}), f32[16,16,256]{2,1,0:T(8,128)S(1)}, u32[]{:S(2)}, u32[]{:S(2)}) async-start(f32[16,16,256]{2,1,0:T(8,128)} %bitcast.13), calls=%async_computation.4 | async-start | bytes 524288 | tf_op jit(solution)/shard_map/all_to_all | solution.py:633
  84.8 12.1 %backward_scans.3 = (f32[256,128]{1,0:T(8,128)S(1)}, f32[520,128]{1,0:T(8,128)S(1)}) custom-call(f32[256,128]{1,0:T(8,128)S(1)} %bitcast.34, f32[1,128]{1,0:T(1,128)S(1)} %bitcast.42, bf16[128,512]{1,0:T(8,128)(2,1)S(1)} %copy-done, bf16[160,256]{1,0:T(8,128)(2,1)S(1)} %bitcast.46, f32[4,8,256]{2,1,0:T(8,128)S(1)} %copy-done.9, f32[4,256]{1,0:T(4,128)S(1)} %copy-done.10, ...), custom_call_target="tpu_custom_call" | custom-call | flops 6442450944 | bytes 524288 | tf_op jit(solution)/shard_map/backward_scans/pallas_call | solution.py:730
  96.9 12.1 %backward_scans.2 = (f32[256,128]{1,0:T(8,128)S(1)}, f32[520,128]{1,0:T(8,128)S(1)}) custom-call(f32[256,128]{1,0:T(8,128)S(1)} %bitcast.32, f32[1,128]{1,0:T(1,128)S(1)} %bitcast.43, bf16[128,512]{1,0:T(8,128)(2,1)S(1)} %copy-done, bf16[160,256]{1,0:T(8,128)(2,1)S(1)} %bitcast.47, f32[4,8,256]{2,1,0:T(8,128)S(1)} %copy-done.9, f32[4,256]{1,0:T(4,128)S(1)} %copy-done.10, ...), custom_call_target="tpu_custom_call" | custom-call | flops 6442450944 | bytes 524288 | tf_op jit(solution)/shard_map/backward_scans/pallas_call | solution.py:730
  109.1 0.1 pack.1
  109.1 17.1 %all_to_all.48 = f32[16,104,128]{2,1,0:T(8,128)S(1)} all-to-all(f32[16,104,128]{2,1,0:T(8,128)S(1)} %pack.1), channel_id=1, replica_groups=mesh['row'=16,'col'=16] {'row'}, dimensions={0} | all-to-all | bytes 1703936 | tf_op jit(solution)/shard_map/all_to_all | solution.py:776
  126.4 31.1 %all_to_all.49 = f32[16,104,128]{2,1,0:T(8,128)S(1)} all-to-all(f32[16,104,128]{2,1,0:T(8,128)S(1)} %pad_maximum_fusion), channel_id=1, replica_groups=mesh['row'=16,'col'=16] {'col'}, dimensions={0} | all-to-all | bytes 1703936 | tf_op jit(solution)/shard_map/all_to_all | solution.py:780
  157.6 0.9 broadcast_in_dim.5
  158.5 6.3 %all-to-all-start.8 = ((f32[16,88,128]{2,1,0:T(8,128)}), f32[16,88,128]{2,1,0:T(8,128)S(1)}, u32[]{:S(2)}, u32[]{:S(2)}) async-start(f32[16,88,128]{2,1,0:T(8,128)} %broadcast_in_dim.5), calls=%async_computation.8 | async-start | bytes 1441792 | tf_op jit(solution)/shard_map/all_to_all | solution.py:639
  164.8 0.7 finish.1
  165.5 11.6 %all-to-all-done.8 = f32[16,88,128]{2,1,0:T(8,128)S(1)} async-done(((f32[16,88,128]{2,1,0:T(8,128)}), f32[16,88,128]{2,1,0:T(8,128)S(1)}, u32[]{:S(2)}, u32[]{:S(2)}) %all-to-all-start.8) | async-done | bytes 720928 | tf_op jit(solution)/shard_map/all_to_all | solution.py:639
  177.2 0.9 unpack.1
  (30 shorter events, 0.3 us)
Async XLA Ops:
  0.6 0.9 copy-start.4
  0.7 0.9 copy-start.1
  2.5 27.2 %copy-start.8 = (f32[4,16,256]{2,1,0:T(8,128)S(1)}, f32[4,16,256]{2,1,0:T(8,128)}, u32[]{:S(2)}) copy-start(f32[4,16,256]{2,1,0:T(8,128)} %decay_log.7) | copy-start | bytes 196612
  22.9 6.8 %copy-start = (bf16[128,512]{1,0:T(8,128)(2,1)S(1)}, bf16[128,512]{1,0:T(8,128)(2,1)}, u32[]{:S(2)}) copy-start(bf16[128,512]{1,0:T(8,128)(2,1)} %in_weight.9) | copy-start | bytes 393220
  22.9 6.8 %copy-start.7 = (bf16[256,160]{0,1:T(8,128)(2,1)S(1)}, bf16[256,160]{0,1:T(8,128)(2,1)}, u32[]{:S(2)}) copy-start(bf16[256,160]{0,1:T(8,128)(2,1)} %param.19) | copy-start | bytes 245764
  22.9 6.8 %copy-start.9 = (f32[4,8,256]{2,1,0:T(8,128)S(1)}, f32[4,8,256]{2,1,0:T(8,128)}, u32[]{:S(2)}) copy-start(f32[4,8,256]{2,1,0:T(8,128)} %step_weight.7) | copy-start | bytes 98308
  22.9 6.8 %copy-start.11 = (f32[4,256]{1,0:T(4,128)S(1)}, f32[4,256]{1,0:T(4,128)}, u32[]{:S(2)}) copy-start(f32[4,256]{1,0:T(4,128)} %skip_gain.7) | copy-start | bytes 12292
  23.0 15.4 %all-to-all-start.1 = ((f32[16,16,128]{2,1,0:T(8,128)}), f32[16,16,128]{2,1,0:T(8,128)S(1)}, u32[]{:S(2)}, u32[]{:S(2)}) async-start(f32[16,16,128]{2,1,0:T(8,128)} %bitcast.7), calls=%async_computation.1 | async-start | bytes 262144 | tf_op jit(solution)/shard_map/all_to_all | solution.py:633
  29.7 0.7 copy-start.10
  29.7 0.7 copy-start.6
  38.4 14.1 %all-to-all-start.2 = ((f32[16,16,256]{2,1,0:T(8,128)}), f32[16,16,256]{2,1,0:T(8,128)S(1)}, u32[]{:S(2)}, u32[]{:S(2)}) async-start(f32[16,16,256]{2,1,0:T(8,128)} %bitcast.9), calls=%async_computation.2 | async-start | bytes 524288 | tf_op jit(solution)/shard_map/all_to_all | solution.py:633
  52.5 14.4 %copy-start.2 = (bf16[256,128]{1,0:T(8,128)(2,1)S(1)}, bf16[256,128]{1,0:T(8,128)(2,1)}, u32[]{:S(2)}) copy-start(bf16[256,128]{1,0:T(8,128)(2,1)} %output_weight.1) | copy-start | bytes 196612
  52.5 14.4 %copy-start.3 = (bf16[16,16,128]{2,1,0:T(8,128)(2,1)S(1)}, bf16[16,16,128]{2,1,0:T(8,128)(2,1)}, u32[]{:S(2)}) copy-start(bf16[16,16,128]{2,1,0:T(8,128)(2,1)} %param.15) | copy-start | bytes 196612
  66.8 0.7 copy-start.5
  79.6 17.3 %all-to-all-start.4 = ((f32[16,16,256]{2,1,0:T(8,128)}), f32[16,16,256]{2,1,0:T(8,128)S(1)}, u32[]{:S(2)}, u32[]{:S(2)}) async-start(f32[16,16,256]{2,1,0:T(8,128)} %bitcast.13), calls=%async_computation.4 | async-start | bytes 524288 | tf_op jit(solution)/shard_map/all_to_all | solution.py:633
  158.5 18.7 %all-to-all-start.8 = ((f32[16,88,128]{2,1,0:T(8,128)}), f32[16,88,128]{2,1,0:T(8,128)S(1)}, u32[]{:S(2)}, u32[]{:S(2)}) async-start(f32[16,88,128]{2,1,0:T(8,128)} %broadcast_in_dim.5), calls=%async_computation.8 | async-start | bytes 1441792 | tf_op jit(solution)/shard_map/all_to_all | solution.py:639
